TPU v7x, 32 devices: a whole 2x2x4 slice. The times are simulated.
32 devices in a mesh: dp: 4 (over z), seq: 8 (over y, x, core).
Axes of the slice: x: 2, y: 2, z: 4, core: 2. Of those that a mesh axis runs over, the one named last changes fastest.
Arguments:
- embeddings: bfloat16 [4, 1024, 1536], P('dp', 'seq'), may hold values from -6 to 6
- conv_one: bfloat16 [3, 1536, 1536], P(None, 'dp'), may hold values from -0.09375 to 0.09375
- conv_two: bfloat16 [3, 1536, 1536], P(None, 'dp'), may hold values from -0.09375 to 0.09375
- head_weight: bfloat16 [1536, 3072], P(None, 'dp'), may hold values from -4 to 4
- counts: int32 [4, 1024, 3072], P(None, 'seq', 'dp'), may hold values from 0 to 12
- dilation: int32 [2], replicated, may hold values from 1 to 32, as said below
Outputs:
- track_loss: float32 [4, 3072], P(None, 'dp')
- grad_head: float32 [1536, 3072], P('seq', 'dp')
- grad_one: float32 [3, 1536, 1536], P(None, 'seq', 'dp')
- grad_two: float32 [3, 1536, 1536], P(None, 'seq', 'dp')
Inputs may be any that keep to these rules, and one draw needn't show every extreme that they name: One of the two convolutions has dilation 32, the other a smaller one.
All inputs are finite; a program needn't handle non-finite values.
Results may differ from a plain program's by a relative error of at most 0.019.
The roundings to bfloat16 on the way count: a program that leaves them out, or rounds other values in their place, can miss the bound.
Values may be sent and summed in bfloat16 or wider, within the bound.
No kernel may reach another device: no remote copies, remote signals or barrier semaphores. Data moves between devices by JAX's collectives and lax.ppermute only.
A program may use at most 128 MiB of HBM per device.

v0:
```python
import jax
import jax.numpy as jnp
from jax import lax
from jax.sharding import PartitionSpec as P

DMAX = 32


def with_halo(value, sides, width):
    for axis, dim in sides:
        size, length = (lax.axis_size(axis), value.shape[dim])
        up = [(i, (i + 1) % size) for i in range(size - 1)]
        down = [(j, i) for i, j in up]
        last = lax.slice_in_dim(value, length - width, length, axis=dim)
        first = lax.slice_in_dim(value, 0, width, axis=dim)
        before = lax.ppermute(last, axis, up)
        after = lax.ppermute(first, axis, down)
        value = jnp.concatenate([before, value, after], axis=dim)
    return value


def combined_all(part, axis, combine):
    gathered = jax.tree.map(lambda a: lax.all_gather(a, axis), part)

    def take(source):
        return jax.tree.map(lambda a: lax.dynamic_index_in_dim(a, source, 0, False), gathered)

    return lax.fori_loop(
        1, lax.axis_size(axis), lambda source, state: combine(state, take(source)), take(0)
    )


def activate(value):
    return jax.nn.gelu(value)


def framed_input(block):
    gathered = lax.all_gather(block, "dp", axis=0, tiled=True)
    framed = with_halo(gathered, (("seq", 1),), DMAX)
    return framed


def framed_hidden(block):
    gathered = lax.all_gather(block, "dp", axis=2, tiled=True)
    framed = with_halo(gathered, (("seq", 1),), DMAX)
    return framed


def shifted_taps(padded, spacing, length, sign):
    return [
        lax.dynamic_slice_in_dim(padded, DMAX + sign * (tap_index - 1) * spacing, length, 1)
        for tap_index in range(3)
    ]


def conv_apply(padded, weight, spacing, length):
    tap_list = shifted_taps(padded, spacing, length, 1)
    running = jnp.einsum("blc,dc->bld", tap_list[0], weight[0], preferred_element_type=jnp.float32)
    for tap_index in (1, 2):
        running = running + jnp.einsum(
            "blc,dc->bld",
            tap_list[tap_index],
            weight[tap_index],
            preferred_element_type=jnp.float32,
        )
    return running


def weight_grad(padded, upstream, spacing, length):
    tap_list = shifted_taps(padded, spacing, length, 1)
    stacked = jnp.stack(
        [
            jnp.einsum("blc,bld->cd", tap_rows, upstream, preferred_element_type=jnp.float32)
            for tap_rows in tap_list
        ]
    )
    return lax.psum_scatter(stacked, "seq", scatter_dimension=1, tiled=True)


def combine_stats(first_stats, second_stats):
    upper = jnp.maximum(first_stats[0], second_stats[0])
    exp_sum = first_stats[1] * jnp.exp(first_stats[0] - upper) + second_stats[1] * jnp.exp(
        second_stats[0] - upper
    )
    return (upper, exp_sum, first_stats[2] + second_stats[2], first_stats[3] + second_stats[3])


def on_device(embeddings, conv_one, conv_two, head_weight, counts, dilation):
    length = embeddings.shape[1]
    chan_dev = conv_one.shape[1]
    own_index = lax.axis_index("dp")
    first_gap = dilation[0]
    second_gap = dilation[1]
    framed_in = framed_input(embeddings)
    pre_one = conv_apply(framed_in, conv_one, first_gap, length)
    centre_in = lax.dynamic_slice_in_dim(framed_in, DMAX, length, 1)
    own_in = lax.dynamic_slice_in_dim(centre_in, own_index * chan_dev, chan_dev, 2)
    hidden_one = (own_in.astype(jnp.float32) + activate(pre_one)).astype(jnp.bfloat16)
    framed_one = framed_hidden(hidden_one)
    pre_two = conv_apply(framed_one, conv_two, second_gap, length)
    hidden_two = (hidden_one.astype(jnp.float32) + activate(pre_two)).astype(jnp.bfloat16)
    head_rows = lax.all_gather(hidden_two, "dp", axis=2, tiled=True)
    logits = jnp.einsum("blc,ct->blt", head_rows, head_weight, preferred_element_type=jnp.float32)
    targets = counts.astype(jnp.float32)
    local_peak = jnp.max(logits, axis=1)
    count_local = jnp.sum(targets, axis=1)
    cross_local = jnp.sum(targets * logits, axis=1)
    exp_local = jnp.sum(jnp.exp(logits - local_peak[:, None, :]), axis=1)
    peak_all, exp_total, count_total, cross_total = combined_all(
        (local_peak, exp_local, count_local, cross_local), "seq", combine_stats
    )
    all_bins = length * lax.axis_size("seq")
    log_total = peak_all + jnp.log(exp_total)
    track_loss = (count_total * log_total - cross_total) / all_bins
    logit_grad = (
        (count_total[:, None, :] * jnp.exp(logits - log_total[:, None, :]) - targets) / all_bins
    ).astype(jnp.bfloat16)
    grad_head = lax.psum_scatter(
        jnp.einsum("blc,blt->ct", head_rows, logit_grad, preferred_element_type=jnp.float32),
        "seq",
        scatter_dimension=0,
        tiled=True,
    )
    back_partial = jnp.einsum(
        "blt,ct->blc", logit_grad, head_weight, preferred_element_type=jnp.float32
    )
    grad_two_out = lax.psum_scatter(
        back_partial.astype(jnp.bfloat16), "dp", scatter_dimension=2, tiled=True
    ).astype(jnp.float32)
    upstream_two = jax.vjp(activate, pre_two)[1](grad_two_out)[0].astype(jnp.bfloat16)
    grad_two = weight_grad(framed_one, upstream_two, second_gap, length)
    framed_back = with_halo(upstream_two, (("seq", 1),), DMAX)
    back_taps = shifted_taps(framed_back, second_gap, length, -1)
    conv_partial = jnp.einsum(
        "bld,dc->blc", back_taps[0], conv_two[0], preferred_element_type=jnp.float32
    )
    for tap_index in (1, 2):
        conv_partial = conv_partial + jnp.einsum(
            "bld,dc->blc",
            back_taps[tap_index],
            conv_two[tap_index],
            preferred_element_type=jnp.float32,
        )
    grad_one_out = grad_two_out + lax.psum_scatter(
        conv_partial.astype(jnp.bfloat16), "dp", scatter_dimension=2, tiled=True
    ).astype(jnp.float32)
    upstream_one = jax.vjp(activate, pre_one)[1](grad_one_out)[0].astype(jnp.bfloat16)
    grad_one = weight_grad(framed_in, upstream_one, first_gap, length)
    return (track_loss, grad_head, grad_one, grad_two)


def solution(mesh):
    placed = (
        P("dp", "seq", None),
        P(None, "dp", None),
        P(None, "dp", None),
        P(None, "dp"),
        P(None, "seq", "dp"),
        P(),
    )
    return jax.shard_map(
        on_device,
        mesh=mesh,
        in_specs=placed,
        out_specs=(P(None, "dp"), P("seq", "dp"), P(None, "seq", "dp"), P(None, "seq", "dp")),
        check_vma=False,
    )
```

profile of v0, /device:TPU:0, one launch (start us, length us, event | category | flops | bytes accessed | tf_op | source)
XLA Modules:
  0.0 506.0 jit_solution(7902621631542485066)
XLA Ops:
  8.0 41.4 %all-gather.12.cloned.1.call-done = bf16[4,128,1536]{2,1,0:T(8,128)(2,1)} async-done(((bf16[1,128,1536]{2,1,0:T(8,128)(2,1)}), bf16[4,128,1536]{2,1,0:T(8,128)(2,1)}) %all-gather.12.cloned.1.call-update) | async-done | bytes 1572880 | tf_op jit(solution)/shard_map/all_gather | solution.py:38
  57.0 2.7 fusion.41
  65.0 40.6 %all-gather.14.cloned.1.call-done = bf16[4,128,1536]{2,1,0:T(8,128)(2,1)} async-done(((bf16[4,128,384]{2,1,0:T(8,128)(2,1)}), bf16[4,128,1536]{2,1,0:T(8,128)(2,1)}) %all-gather.14.cloned.1.call-update) | async-done | bytes 1572880 | tf_op jit(solution)/shard_map/all_gather | solution.py:44
  111.5 2.7 fusion.36
  119.4 41.0 %all-gather.16.cloned.1.call-done = bf16[4,128,1536]{2,1,0:T(8,128)(2,1)} async-done(((bf16[4,128,384]{2,1,0:T(8,128)(2,1)}), bf16[4,128,1536]{2,1,0:T(8,128)(2,1)}) %all-gather.16.cloned.1.call-update) | async-done | bytes 1572880 | tf_op jit(solution)/shard_map/all_gather | solution.py:102
  160.4 2.9 fusion.86
  163.3 9.2 %all-gather.4 = f32[8,4,768]{2,1,0:T(4,128)S(1)} all-gather(f32[1,4,768]{2,1,0:T(4,128)S(1)} %bitcast.138), channel_id=2, replica_groups=mesh['dp'=4,'seq'=8] {'seq'}, dimensions={0}, use_global_device_ids=true | all-gather | bytes 110592 | tf_op jit(solution)/shard_map/all_gather | solution.py:23
  173.0 9.2 %all-gather.5 = f32[8,4,768]{2,1,0:T(4,128)S(1)} all-gather(f32[1,4,768]{2,1,0:T(4,128)S(1)} %bitcast.140), channel_id=3, replica_groups=mesh['dp'=4,'seq'=8] {'seq'}, dimensions={0}, use_global_device_ids=true | all-gather | bytes 110592 | tf_op jit(solution)/shard_map/all_gather | solution.py:23
  182.2 8.3 %all-gather.6 = f32[8,4,768]{2,1,0:T(4,128)S(1)} all-gather(f32[1,4,768]{2,1,0:T(4,128)S(1)} %bitcast.139), channel_id=4, replica_groups=mesh['dp'=4,'seq'=8] {'seq'}, dimensions={0}, use_global_device_ids=true | all-gather | bytes 110592 | tf_op jit(solution)/shard_map/all_gather | solution.py:23
  190.5 9.4 %all-gather.7 = f32[8,4,768]{2,1,0:T(4,128)S(1)} all-gather(f32[1,4,768]{2,1,0:T(4,128)S(1)} %bitcast.137), channel_id=5, replica_groups=mesh['dp'=4,'seq'=8] {'seq'}, dimensions={0}, use_global_device_ids=true | all-gather | bytes 110592 | tf_op jit(solution)/shard_map/all_gather | solution.py:23
  200.5 5.5 %while.21 = (s32[]{:T(128)}, f32[4,768]{1,0:T(4,128)S(1)}, f32[4,768]{1,0:T(4,128)S(1)}, f32[4,768]{1,0:T(4,128)S(1)}, f32[4,768]{1,0:T(4,128)S(1)}, /*index=5*/...) while((s32[]{:T(128)}, f32[4,768]{1,0:T(4,128)S(1)}, ...), condition=%wide.region_5.6_spmd, body=%wide.region_4.5_spmd.sunk | while | flops 24581 | bytes 147623 | solution.py:28
  212.3 2.7 copy.35
  216.6 33.5 %reduce-scatter.16.cloned.1.call-done = bf16[384,512]{1,0:T(8,128)(2,1)} async-done(((bf16[1536,512]{1,0:T(8,128)(2,1)}), bf16[384,512]{1,0:T(8,128)(2,1)}) %reduce-scatter.16.cloned.1.call-update) | async-done | bytes 393232
  253.3 3.3 collective-permute-start.4
  263.2 2.9 copy.43
  266.2 5.0 convolution_bitcast_fusion
  271.3 2.6 convolution_bitcast_fusion.1
  276.3 3.3 pad_maximum_fusion.1
  279.9 22.8 %reduce-scatter.18.cloned.1.call-done = bf16[384,512]{1,0:T(8,128)(2,1)} async-done(((bf16[1536,512]{1,0:T(8,128)(2,1)}), bf16[384,512]{1,0:T(8,128)(2,1)}) %reduce-scatter.18.cloned.1.call-update) | async-done | bytes 393232
  304.8 2.6 convolution_bitcast_fusion.4
  309.8 3.5 pad_maximum_fusion
  313.4 46.1 %reduce-scatter.10.cloned.1.call-done = f32[192,768]{1,0:T(8,128)} async-done(((f32[1536,768]{1,0:T(8,128)}), f32[192,768]{1,0:T(8,128)}) %reduce-scatter.10.cloned.1.call-update) | async-done | bytes 589840 | tf_op jit(solution)/shard_map/reduce_scatter | solution.py:118
  359.5 70.0 %reduce-scatter.14.cloned.1.call-done = f32[3,192,384]{2,1,0:T(8,128)} async-done(((f32[3,1536,384]{2,1,0:T(8,128)}), f32[3,192,384]{2,1,0:T(8,128)}) %reduce-scatter.14.cloned.1.call-update) | async-done | bytes 884752 | tf_op jit(solution)/shard_map/reduce_scatter | solution.py:77
  429.5 69.6 %reduce-scatter.12.cloned.1.call-done = f32[3,192,384]{2,1,0:T(8,128)} async-done(((f32[3,1536,384]{2,1,0:T(8,128)}), f32[3,192,384]{2,1,0:T(8,128)}) %reduce-scatter.12.cloned.1.call-update) | async-done | bytes 884752 | tf_op jit(solution)/shard_map/reduce_scatter | solution.py:77
  (119 shorter events, 51.9 us)
Async XLA Ops:
  7.2 153.2 %copy-start = (bf16[1536,768]{1,0:T(8,128)(2,1)S(1)}, bf16[1536,768]{1,0:T(8,128)(2,1)}, u32[]{:S(2)}) copy-start(bf16[1536,768]{1,0:T(8,128)(2,1)} %param.11) | copy-start | bytes 7077892
  7.2 42.2 %all-gather.12.cloned.1.call-start = ((), (), s32[]{:S(2)}) async-start(), calls=%async_computation.5 | async-start | bytes 1966080 | tf_op jit(solution)/shard_map/all_gather | solution.py:38
  7.9 97.7 %all-gather.14.cloned.1.call-start = ((), (), s32[]{:S(2)}) async-start(), calls=%async_computation.6 | async-start | bytes 1966080 | tf_op jit(solution)/shard_map/all_gather | solution.py:44
  50.6 9.1 %collective-permute-start = (bf16[4,32,1536]{2,1,0:T(8,128)(2,1)S(1)}, bf16[4,32,1536]{2,1,0:T(8,128)(2,1)S(1)}, u32[]{:S(2)}, u32[]{:S(2)}) collective-permute-start(bf16[4,32,1536]{2,1,0:T(8,128)(2,1)S(1)} %get-tuple-element.261), channel_id=1, source_target_pairs={{0,1},{1,2},{2,3},{3,4},{4,5},{5,6},{6,7},{8,9},{9,10},{10,11},{11... | collective-permute-start | bytes 1179656 | tf_op jit(solution)/shard_map/ppermute | solution.py:16
  55.5 4.2 copy-start.4
  55.5 5.1 %collective-permute-start.1 = (bf16[4,32,1536]{2,1,0:T(8,128)(2,1)S(1)}, bf16[4,32,1536]{2,1,0:T(8,128)(2,1)S(1)}, u32[]{:S(2)}, u32[]{:S(2)}) collective-permute-start(bf16[4,32,1536]{2,1,0:T(8,128)(2,1)S(1)} %get-tuple-element.260), channel_id=1, source_target_pairs={{1,0},{2,1},{3,2},{4,3},{5,4},{6,5},{7,6},{9,8},{10,9},{11,10},{12... | collective-permute-start | bytes 1179656 | tf_op jit(solution)/shard_map/ppermute | solution.py:17
  61.7 3.2 copy-start.15
  65.0 95.4 %all-gather.16.cloned.1.call-start = ((), (), s32[]{:S(2)}) async-start(), calls=%async_computation.7 | async-start | bytes 1966080 | tf_op jit(solution)/shard_map/all_gather | solution.py:102
  106.8 7.5 %collective-permute-start.2 = (bf16[4,32,1536]{2,1,0:T(8,128)(2,1)S(1)}, bf16[4,32,1536]{2,1,0:T(8,128)(2,1)S(1)}, u32[]{:S(2)}, u32[]{:S(2)}) collective-permute-start(bf16[4,32,1536]{2,1,0:T(8,128)(2,1)S(1)} %get-tuple-element.259), channel_id=1, source_target_pairs={{0,1},{1,2},{2,3},{3,4},{4,5},{5,6},{6,7},{8,9},{9,10},{10,11},{11... | collective-permute-start | bytes 1179656 | tf_op jit(solution)/shard_map/ppermute | solution.py:16
  110.1 4.2 copy-start.2
  110.1 5.4 %collective-permute-start.3 = (bf16[4,32,1536]{2,1,0:T(8,128)(2,1)S(1)}, bf16[4,32,1536]{2,1,0:T(8,128)(2,1)S(1)}, u32[]{:S(2)}, u32[]{:S(2)}) collective-permute-start(bf16[4,32,1536]{2,1,0:T(8,128)(2,1)S(1)} %get-tuple-element.258), channel_id=1, source_target_pairs={{1,0},{2,1},{3,2},{4,3},{5,4},{6,5},{7,6},{9,8},{10,9},{11,10},{12... | collective-permute-start | bytes 1179656 | tf_op jit(solution)/shard_map/ppermute | solution.py:17
  116.3 3.0 copy-start.17
  119.3 130.7 %reduce-scatter.16.cloned.1.call-start = ((), (), s32[]{:S(2)}) async-start(), calls=%async_computation.11 | async-start | bytes 1966080
  160.4 12.1 %copy-start.6 = (s32[4,128,768]{2,1,0:T(8,128)S(1)}, s32[4,128,768]{2,1,0:T(8,128)}, u32[]{:S(2)}) copy-start(s32[4,128,768]{2,1,0:T(8,128)} %param.12) | copy-start | bytes 4718596
  163.3 9.7 %copy-start.7 = (f32[4,128,768]{2,1,0:T(8,128)}, f32[4,128,768]{2,1,0:T(8,128)S(1)}, u32[]{:S(2)}) copy-start(f32[4,128,768]{2,1,0:T(8,128)S(1)} %get-tuple-element.271) | copy-start | bytes 4718596
  216.5 86.2 %reduce-scatter.18.cloned.1.call-start = ((), (), s32[]{:S(2)}) async-start(), calls=%async_computation.12 | async-start | bytes 1966080
  252.0 6.9 %collective-permute-start.5 = (bf16[4,32,384]{2,1,0:T(8,128)(2,1)S(1)}, bf16[4,32,384]{2,1,0:T(8,128)(2,1)S(1)}, u32[]{:S(2)}, u32[]{:S(2)}) collective-permute-start(bf16[4,32,384]{2,1,0:T(8,128)(2,1)S(1)} %get-tuple-element.263), channel_id=1, source_target_pairs={{1,0},{2,1},{3,2},{4,3},{5,4},{6,5},{7,6},{9,8},{10,9},{11,10},{12... | collective-permute-start | bytes 294920 | tf_op jit(solution)/shard_map/ppermute | solution.py:17
  253.3 5.7 %copy-start.9 = (bf16[3,384,1536]{2,1,0:T(8,128)(2,1)S(1)}, bf16[3,384,1536]{2,1,0:T(8,128)(2,1)}, u32[]{:S(2)}) copy-start(bf16[3,384,1536]{2,1,0:T(8,128)(2,1)} %param.10) | copy-start | bytes 10616836
  253.3 5.6 %collective-permute-start.4 = (bf16[4,32,384]{2,1,0:T(8,128)(2,1)S(1)}, bf16[4,32,384]{2,1,0:T(8,128)(2,1)S(1)}, u32[]{:S(2)}, u32[]{:S(2)}) collective-permute-start(bf16[4,32,384]{2,1,0:T(8,128)(2,1)S(1)} %get-tuple-element.262), channel_id=1, source_target_pairs={{0,1},{1,2},{2,3},{3,4},{4,5},{5,6},{6,7},{8,9},{9,10},{10,11},{11... | collective-permute-start | bytes 294920 | tf_op jit(solution)/shard_map/ppermute | solution.py:16
  266.2 93.4 %reduce-scatter.10.cloned.1.call-start = ((), (), s32[]{:S(2)}) async-start(), calls=%async_computation.8 | async-start | bytes 5308416 | tf_op jit(solution)/shard_map/reduce_scatter | solution.py:118
  271.2 158.3 %reduce-scatter.14.cloned.1.call-start = ((), (), s32[]{:S(2)}) async-start(), calls=%async_computation.10 | async-start | bytes 7962624 | tf_op jit(solution)/shard_map/reduce_scatter | solution.py:77
  279.6 24.5 %copy-start.10 = (f32[4,128,384]{2,1,0:T(8,128)S(1)}, f32[4,128,384]{2,1,0:T(8,128)}, u32[]{:S(2)}) copy-start(f32[4,128,384]{2,1,0:T(8,128)} %get-tuple-element.267) | copy-start | bytes 2359300
  279.7 219.5 %reduce-scatter.12.cloned.1.call-start = ((), (), s32[]{:S(2)}) async-start(), calls=%async_computation.9 | async-start | bytes 7962624 | tf_op jit(solution)/shard_map/reduce_scatter | solution.py:77
  313.4 185.8 %copy-start.1 = (bf16[1536,768]{1,0:T(8,128)(2,1)S(1)}, bf16[1536,768]{1,0:T(8,128)(2,1)}, u32[]{:S(2)}) copy-start(bf16[1536,768]{1,0:T(8,128)(2,1)} %param.11) | copy-start | bytes 7077892
  (10 other events, 19.4 us)
Sparse Core Ops, SparseCore 0:
  9.6 39.7 all-gather.11
  65.1 40.5 all-gather.13
  119.4 40.9 all-gather.15
  216.6 33.3 reduce-scatter.15
  266.3 36.4 reduce-scatter.17
  306.6 52.8 reduce-scatter.9
  364.0 65.4 reduce-scatter.13
  433.6 65.4 reduce-scatter.11
where the time goes:
time: 507 us; the launch traced here: 506 us
  waiting for transfers between devices  368 us (73%)
  blocking collectives  36 us (7%)
  matrix products  35.7 us (7%)
  local copies, waits for them, and re-layouts  20.2 us (4%)
  between operations  18.5 us (4%)
  other arithmetic  16.8 us (3%)
  starting transfers between devices  10.9 us (2%)
    reduce_scatter x2, waiting for transfers between devices, weight_grad(): return lax.psum_scatter(stacked, 'seq', scatter_dimension=1, tiled=True)  140 us
    unnamed x10, waiting for transfers between devices  57.1 us
    reduce_scatter x1, waiting for transfers between devices, on_device(): lax.psum_scatter(jnp.einsum('blc,blt->ct', head_rows, logit_grad, preferr...  46.1 us
    all_gather x1, waiting for transfers between devices, framed_input(): gathered = lax.all_gather(block, 'dp', axis=0, tiled=True)  41.4 us
    all_gather x1, waiting for transfers between devices, on_device(): head_rows = lax.all_gather(hidden_two, 'dp', axis=2, tiled=True)  41 us
    all_gather x1, waiting for transfers between devices, framed_hidden(): gathered = lax.all_gather(block, 'dp', axis=2, tiled=True)  40.6 us
    all_gather x4, blocking collectives, combined_all(): gathered = jax.tree.map(lambda a: lax.all_gather(a, axis), part)  36 us
    unnamed x52, local copies, waits for them, and re-layouts  16.4 us
  transfers between devices with their start and end apart: 14, of which 10 were waited for; matrix products, arithmetic and copies ran while one was open for 6% of the time, Pallas kernels for 0%

commit v1 on v0

v1 whole, which is shorter than its diff:
```python
import jax
import jax.numpy as jnp
from jax import lax
from jax.sharding import PartitionSpec as P

DMAX = 32
GROUPS = 1
F32 = jnp.float32
BF16 = jnp.bfloat16


def dot(spec, a, b):
    return jnp.einsum(spec, a, b, preferred_element_type=F32)


def activate(value):
    return jax.nn.gelu(value)


def activate_grad(pre, upstream):
    return jax.vjp(activate, pre)[1](upstream)[0]


def send(value, axis, pairs):
    return lax.ppermute(value, axis, pairs)


def swap(value, axis, mask):
    return send(value, axis, [(i, i ^ mask) for i in range(lax.axis_size(axis))])


def line_gather(block):
    size = lax.axis_size("dp")
    if size != 4:
        return [block] + [swap(block, "dp", m) for m in range(1, size)]
    far = swap(block, "dp", 2)
    near = swap(block, "dp", 1)
    inner = send(block, "dp", [(1, 2), (2, 1)])
    outer = send(far, "dp", [(2, 3), (1, 0)])
    place = lax.axis_index("dp")
    middle = (place == 1) | (place == 2)
    return [block, near, far, jnp.where(middle, inner, outer)]


def line_scatter(chunks):
    size = lax.axis_size("dp")
    total = chunks[0].astype(F32)
    if size != 4:
        for m in range(1, size):
            total = total + swap(chunks[m], "dp", m).astype(F32)
        return total
    passed = send(chunks[3], "dp", [(0, 1), (3, 2)])
    near = swap(chunks[1], "dp", 1)
    far_chunk = (chunks[2].astype(F32) + passed.astype(F32)).astype(BF16)
    far = swap(far_chunk, "dp", 2)
    inner = send(chunks[3], "dp", [(1, 2), (2, 1)])
    return total + near.astype(F32) + inner.astype(F32) + far.astype(F32)


def with_halo(value):
    size, length = lax.axis_size("seq"), value.shape[1]
    up = [(i, i + 1) for i in range(size - 1)]
    down = [(j, i) for i, j in up]
    before = send(value[:, length - DMAX :], "seq", up)
    after = send(value[:, :DMAX], "seq", down)
    return jnp.concatenate([before, value, after], axis=1)


def shifted_taps(padded, spacing, sign):
    length = padded.shape[1] - 2 * DMAX
    return [
        lax.dynamic_slice_in_dim(padded, DMAX + sign * (tap - 1) * spacing, length, 1)
        for tap in range(3)
    ]


def conv_apply(padded, weight, spacing, sign, spec):
    taps = shifted_taps(padded, spacing, sign)
    total = dot(spec, taps[0], weight[0])
    for tap in (1, 2):
        total = total + dot(spec, taps[tap], weight[tap])
    return total


def by_partner(value, dim):
    size = lax.axis_size("dp")
    width = value.shape[dim] // size
    place = lax.axis_index("dp")
    return jnp.concatenate(
        [lax.dynamic_slice_in_dim(value, (place ^ m) * width, width, dim) for m in range(size)],
        axis=dim,
    )


def pair_rows(value):
    return jnp.concatenate([value, swap(value, "seq", 1)], axis=0)


def pair_channels(value, ordered):
    half = value.shape[-1] // 2
    core = lax.axis_index("seq") % 2
    if ordered:
        core = core ^ (lax.axis_index("dp") // (lax.axis_size("dp") // 2))
    dim = value.ndim - 1
    mine = lax.dynamic_slice_in_dim(value, core * half, half, dim)
    other = lax.dynamic_slice_in_dim(value, (1 - core) * half, half, dim)
    return jnp.concatenate([mine, swap(other, "seq", 1)], axis=0)


def spread_sum(partial, ordered):
    chips = lax.axis_size("seq") // 2
    rows = partial.shape[1] // chips
    place, layer = lax.axis_index("seq"), lax.axis_index("dp")
    width = 2 * partial.shape[1] // lax.axis_size("dp")
    total = None
    for j in range(chips):
        target = (place // 2) ^ j
        offset = target * rows
        if ordered:
            group = (offset // width) ^ (layer % (lax.axis_size("dp") // 2))
            offset = group * width + offset % width
        block = lax.dynamic_slice_in_dim(partial, offset, rows, 1)
        pairs = [(s, (s % 2) * chips + ((s // 2) ^ j)) for s in range(2 * chips)]
        block = send(block, "seq", pairs).astype(F32)
        total = block if total is None else total + block
    return total


def weight_grad(rows, upstream, spacing, ordered):
    taps = shifted_taps(rows, spacing, 1)
    stacked = jnp.stack([dot("blc,bld->cd", tap, upstream).astype(BF16) for tap in taps])
    return spread_sum(stacked, ordered)


def on_device(embeddings, conv_one, conv_two, head_weight, counts, dilation):
    length = embeddings.shape[1]
    size = lax.axis_size("dp")
    width = conv_one.shape[1]
    batch = counts.shape[0]
    layer = lax.axis_index("dp")
    first_gap, second_gap = dilation[0], dilation[1]
    all_bins = length * lax.axis_size("seq")
    per_layer = embeddings.shape[0]

    def absolute(value):
        stacked = value.reshape((size, per_layer) + value.shape[1:])
        picked = [lax.dynamic_index_in_dim(stacked, layer ^ b, 0, False) for b in range(size)]
        return jnp.concatenate(picked, axis=0)

    groups = [slice(i * batch // GROUPS, (i + 1) * batch // GROUPS) for i in range(GROUPS)]

    blocks = line_gather(embeddings)
    frames = [with_halo(block) for block in blocks]
    pre_one_parts, hidden_parts = [], []
    for block, frame in zip(blocks, frames):
        pre = conv_apply(frame, conv_one, first_gap, 1, "blc,dc->bld")
        own = lax.dynamic_slice_in_dim(block, layer * width, width, 2)
        pre_one_parts.append(pre)
        hidden_parts.append((own.astype(F32) + activate(pre)).astype(BF16))
    framed_in = jnp.concatenate(frames, axis=0)
    hidden_one = absolute(jnp.concatenate(hidden_parts, axis=0))
    pre_one = absolute(jnp.concatenate(pre_one_parts, axis=0))

    conv_two_r = by_partner(conv_two, 2)
    head_r = by_partner(head_weight, 0)
    targets = counts.astype(F32)

    framed_one, pre_two, hidden_two = [], [], []
    for g in groups:
        framed = with_halo(jnp.concatenate(line_gather(hidden_one[g]), axis=2))
        pre = conv_apply(framed, conv_two_r, second_gap, 1, "blc,dc->bld")
        framed_one.append(framed)
        pre_two.append(pre)
        hidden_two.append((hidden_one[g].astype(F32) + activate(pre)).astype(BF16))

    head_rows, logits, stats = [], [], []
    for g, hidden in zip(groups, hidden_two):
        rows = jnp.concatenate(line_gather(hidden), axis=2)
        value = dot("blc,ct->blt", rows, head_r)
        peak = jnp.max(value, axis=1)
        total = jnp.sum(jnp.exp(value - peak[:, None, :]), axis=1)
        cross = jnp.sum(targets[g] * value, axis=1)
        head_rows.append(rows)
        logits.append(value)
        stats.append(jnp.stack([peak, total, jnp.sum(targets[g], axis=1), cross]))

    losses, back_two = [], []
    logit_grads = []
    for g, value, stat in zip(groups, logits, stats):
        every = lax.all_gather(stat, "seq")
        peak = jnp.max(every[:, 0], axis=0)
        total = jnp.sum(every[:, 1] * jnp.exp(every[:, 0] - peak), axis=0)
        count_total = jnp.sum(every[:, 2], axis=0)
        cross_total = jnp.sum(every[:, 3], axis=0)
        log_total = peak + jnp.log(total)
        losses.append((count_total * log_total - cross_total) / all_bins)
        logit_grad = (
            (count_total[:, None] * jnp.exp(value - log_total[:, None]) - targets[g]) / all_bins
        ).astype(BF16)
        logit_grads.append(logit_grad)

    grad_two_out, up_two = [], []
    for i, g in enumerate(groups):
        back = dot("blt,ct->blc", logit_grads[i], head_r).astype(BF16)
        grad = line_scatter(jnp.split(back, size, axis=2))
        grad_two_out.append(grad)
        up_two.append(activate_grad(pre_two[i], grad).astype(BF16))

    head_all = pair_channels(jnp.concatenate(head_rows, axis=0), True)
    grad_all = pair_rows(jnp.concatenate(logit_grads, axis=0))
    head_part = dot("blc,blt->ct", head_all, grad_all).astype(BF16)
    grad_head = spread_sum(head_part[None], True)[0]

    up_one = []
    for i, g in enumerate(groups):
        framed = with_halo(up_two[i])
        back = conv_apply(framed, conv_two_r, second_gap, -1, "bld,dc->blc").astype(BF16)
        grad = grad_two_out[i] + line_scatter(jnp.split(back, size, axis=2))
        up_one.append(activate_grad(pre_one[g], grad).astype(BF16))

    one_all = pair_channels(jnp.concatenate(framed_one, axis=0), True)
    grad_two = weight_grad(one_all, pair_rows(jnp.concatenate(up_two, axis=0)), second_gap, True)

    in_all = pair_channels(framed_in, False)
    up_rel = absolute(jnp.concatenate(up_one, axis=0))
    grad_one = weight_grad(in_all, pair_rows(up_rel), first_gap, False)
    return (jnp.concatenate(losses, axis=0), grad_head, grad_one, grad_two)


def solution(mesh):
    placed = (
        P("dp", "seq", None),
        P(None, "dp", None),
        P(None, "dp", None),
        P(None, "dp"),
        P(None, "seq", "dp"),
        P(),
    )
    return jax.shard_map(
        on_device,
        mesh=mesh,
        in_specs=placed,
        out_specs=(P(None, "dp"), P("seq", "dp"), P(None, "seq", "dp"), P(None, "seq", "dp")),
        check_vma=False,
    )
```

time: 507 us -> 308 us (0.61)
  waiting for transfers between devices: 368 us -> 134 us
  starting transfers between devices: 10.9 us -> 91.8 us
  blocking collectives: 36 us -> 18.4 us
  between operations: 18.5 us -> 5.89 us
  local copies, waits for them, and re-layouts: 20.2 us -> 9.01 us
    reduce_scatter x3 -> x0, waiting for transfers between devices: 186 us -> none  [the longest x2 140 us: weight_grad(): return lax.psum_scatter(stacked, 'seq', scatter_dimension=1, tiled=True)]
    ppermute x6 -> x50, waiting for transfers between devices: 1.82 us -> 134 us  [send(): return lax.ppermute(value, axis, pairs)]
    all_gather x3 -> x0, waiting for transfers between devices: 123 us -> none  [the longest x1 41.4 us: framed_input(): gathered = lax.all_gather(block, 'dp', axis=0, tiled=True)]
    ppermute x6 -> x50, starting transfers between devices: 10.4 us -> 91.8 us  [send(): return lax.ppermute(value, axis, pairs)]
    unnamed x10 -> x0, waiting for transfers between devices: 57.1 us -> none
    all_gather x4 -> x1, blocking collectives: 36 us -> 18.4 us  [on_device(): every = lax.all_gather(stat, 'seq')]
    unnamed x52 -> x72, local copies, waits for them, and re-layouts: 16.4 us -> 2.53 us
    another operation x2 -> x3, other arithmetic: 6.86 us -> 0.49 us  [the longest x2 0.47 us: weight_grad(): jnp.stack([dot('blc,bld->cd', tap, upstream).astype(BF16) for tap in taps])]
  transfers between devices with their start and end apart: 14 -> 50, of which waited for: 10 -> 19; matrix products, arithmetic and copies ran while one was open for 6% -> 12% of each run, Pallas kernels for 0% -> 0%
where the time goes in v1:
time: 308 us; the launch traced here: 307 us
  waiting for transfers between devices  134 us (44%)
  starting transfers between devices  91.8 us (30%)
  matrix products  33.2 us (11%)
  blocking collectives  18.4 us (6%)
  other arithmetic  14.3 us (5%)
  local copies, waits for them, and re-layouts  9.01 us (3%)
  between operations  5.89 us (2%)
    ppermute x50, waiting for transfers between devices, send(): return lax.ppermute(value, axis, pairs)  134 us
    ppermute x50, starting transfers between devices, send(): return lax.ppermute(value, axis, pairs)  91.8 us
    dot_general x27, matrix products, dot(): return jnp.einsum(spec, a, b, preferred_element_type=F32)  33.2 us
    all_gather x1, blocking collectives, on_device(): every = lax.all_gather(stat, 'seq')  18.4 us
  transfers between devices with their start and end apart: 50, of which 19 were waited for; matrix products, arithmetic and copies ran while one was open for 12% of the time, Pallas kernels for 0%

profile of v1, /device:TPU:0, one launch (start us, length us, event | category | flops | bytes accessed | tf_op | source)
XLA Modules:
  0.0 307.1 jit_solution(8941103694184047999)
XLA Ops:
  4.4 3.9 %collective-permute-start.5 = (bf16[1,128,1536]{2,1,0:T(8,128)(2,1)}, bf16[1,128,1536]{2,1,0:T(8,128)(2,1)S(1)}, u32[]{:S(2)}, u32[]{:S(2)}) collective-permute-start(bf16[1,128,1536]{2,1,0:T(8,128)(2,1)} %param.6), channel_id=1, source_target_pairs={{0,16},{8,24},{16,0},{24,8},{1,17},{9,25},{17,1},{25,9},{2,18},{10... | collective-permute-start | bytes 1179656 | tf_op jit(solution)/shard_map/ppermute | solution.py:25
  24.9 3.6 %collective-permute-start.3 = (bf16[1,32,1536]{2,1,0:T(8,128)(2,1)S(1)}, bf16[1,32,1536]{2,1,0:T(8,128)(2,1)S(1)}, u32[]{:S(2)}, u32[]{:S(2)}) collective-permute-start(bf16[1,32,1536]{2,1,0:T(8,128)(2,1)S(1)} %get-tuple-element.64), channel_id=1, source_target_pairs={{0,1},{1,2},{2,3},{3,4},{4,5},{5,6},{6,7},{8,9},{9,10},{10,11},{11... | collective-permute-start | bytes 294920 | tf_op jit(solution)/shard_map/ppermute | solution.py:25
  28.5 5.6 %collective-permute-done.5 = bf16[1,128,1536]{2,1,0:T(8,128)(2,1)S(1)} collective-permute-done((bf16[1,128,1536]{2,1,0:T(8,128)(2,1)}, bf16[1,128,1536]{2,1,0:T(8,128)(2,1)S(1)}, u32[]{:S(2)}, u32[]{:S(2)}) %collective-permute-start.5) | collective-permute-done | bytes 393248 | tf_op jit(solution)/shard_map/ppermute | solution.py:25
  43.3 9.5 %collective-permute-done.9 = bf16[1,128,1536]{2,1,0:T(8,128)(2,1)S(1)} collective-permute-done((bf16[1,128,1536]{2,1,0:T(8,128)(2,1)S(1)}, bf16[1,128,1536]{2,1,0:T(8,128)(2,1)S(1)}, u32[]{:S(2)}, u32[]{:S(2)}) %collective-permute-start.9) | collective-permute-done | bytes 393248 | tf_op jit(solution)/shard_map/ppermute | solution.py:25
  69.5 16.3 %collective-permute-done.13 = bf16[4,128,384]{2,1,0:T(8,128)(2,1)} collective-permute-done((bf16[4,128,384]{2,1,0:T(8,128)(2,1)}, bf16[4,128,384]{2,1,0:T(8,128)(2,1)}, u32[]{:S(2)}, u32[]{:S(2)}) %collective-permute-start.13) | collective-permute-done | bytes 393248 | tf_op jit(solution)/shard_map/ppermute | solution.py:25
  89.4 9.6 %collective-permute-done.15 = bf16[4,128,384]{2,1,0:T(8,128)(2,1)} collective-permute-done((bf16[4,128,384]{2,1,0:T(8,128)(2,1)}, bf16[4,128,384]{2,1,0:T(8,128)(2,1)}, u32[]{:S(2)}, u32[]{:S(2)}) %collective-permute-start.15) | collective-permute-done | bytes 393248 | tf_op jit(solution)/shard_map/ppermute | solution.py:25
  106.0 3.4 %collective-permute-done.17 = bf16[4,32,1536]{2,1,0:T(8,128)(2,1)S(1)} collective-permute-done((bf16[4,32,1536]{2,1,0:T(8,128)(2,1)S(1)}, bf16[4,32,1536]{2,1,0:T(8,128)(2,1)S(1)}, u32[]{:S(2)}, u32[]{:S(2)}) %collective-permute-start.17) | collective-permute-done | bytes 393248 | tf_op jit(solution)/shard_map/ppermute | solution.py:25
  117.3 4.7 %collective-permute-start.18 = (bf16[4,128,384]{2,1,0:T(8,128)(2,1)}, bf16[4,128,384]{2,1,0:T(8,128)(2,1)S(1)}, u32[]{:S(2)}, u32[]{:S(2)}) collective-permute-start(bf16[4,128,384]{2,1,0:T(8,128)(2,1)} %get-tuple-element.79), channel_id=1, source_target_pairs={{0,8},{8,0},{16,24},{24,16},{1,9},{9,1},{17,25},{25,17},{2,10},{10... | collective-permute-start | bytes 1179656 | tf_op jit(solution)/shard_map/ppermute | solution.py:25
  122.1 11.3 %collective-permute-done.19 = bf16[4,128,384]{2,1,0:T(8,128)(2,1)} collective-permute-done((bf16[4,128,384]{2,1,0:T(8,128)(2,1)}, bf16[4,128,384]{2,1,0:T(8,128)(2,1)}, u32[]{:S(2)}, u32[]{:S(2)}) %collective-permute-start.19) | collective-permute-done | bytes 393248 | tf_op jit(solution)/shard_map/ppermute | solution.py:25
  135.2 10.1 %collective-permute-done.21 = bf16[4,128,384]{2,1,0:T(8,128)(2,1)S(1)} collective-permute-done((bf16[4,128,384]{2,1,0:T(8,128)(2,1)}, bf16[4,128,384]{2,1,0:T(8,128)(2,1)S(1)}, u32[]{:S(2)}, u32[]{:S(2)}) %collective-permute-start.21) | collective-permute-done | bytes 393248 | tf_op jit(solution)/shard_map/ppermute | solution.py:25
  148.6 18.4 %all-gather = f32[32,4,768]{2,1,0:T(4,128)S(1)} all-gather(f32[4,4,768]{2,1,0:T(4,128)S(1)} %pad_maximum_fusion.18), channel_id=2, replica_groups=mesh['dp'=4,'seq'=8] {'seq'}, dimensions={0}, use_global_device_ids=true | all-gather | bytes 442368 | tf_op jit(solution)/shard_map/all_gather | solution.py:190
  175.8 4.9 %collective-permute-done.31 = bf16[4,128,384]{2,1,0:T(8,128)(2,1)S(1)} collective-permute-done((bf16[4,128,384]{2,1,0:T(8,128)(2,1)S(1)}, bf16[4,128,384]{2,1,0:T(8,128)(2,1)S(1)}, u32[]{:S(2)}, u32[]{:S(2)}) %collective-permute-start.31) | collective-permute-done | bytes 393248 | tf_op jit(solution)/shard_map/ppermute | solution.py:25
  184.9 5.4 %collective-permute-done.29 = bf16[4,128,384]{2,1,0:T(8,128)(2,1)S(1)} collective-permute-done((bf16[4,128,384]{2,1,0:T(8,128)(2,1)S(1)}, bf16[4,128,384]{2,1,0:T(8,128)(2,1)S(1)}, u32[]{:S(2)}, u32[]{:S(2)}) %collective-permute-start.29) | collective-permute-done | bytes 393248 | tf_op jit(solution)/shard_map/ppermute | solution.py:25
  190.3 12.1 %collective-permute-done.32 = bf16[4,128,384]{2,1,0:T(8,128)(2,1)S(1)} collective-permute-done((bf16[4,128,384]{2,1,0:T(8,128)(2,1)S(1)}, bf16[4,128,384]{2,1,0:T(8,128)(2,1)S(1)}, u32[]{:S(2)}, u32[]{:S(2)}) %collective-permute-start.32) | collective-permute-done | bytes 393248 | tf_op jit(solution)/shard_map/ppermute | solution.py:25
  211.5 3.3 %collective-permute-start.28 = (bf16[4,192,768]{2,1,0:T(8,128)(2,1)S(1)}, bf16[4,192,768]{2,1,0:T(8,128)(2,1)S(1)}, u32[]{:S(2)}, u32[]{:S(2)}) collective-permute-start(bf16[4,192,768]{2,1,0:T(8,128)(2,1)S(1)} %get-tuple-element.25), channel_id=1, source_target_pairs={{0,1},{1,0},{2,3},{3,2},{4,5},{5,4},{6,7},{7,6},{8,9},{9,8},{10,11... | collective-permute-start | bytes 3538952 | tf_op jit(solution)/shard_map/ppermute | solution.py:25
  219.3 4.5 %collective-permute-start.35 = (bf16[4,128,384]{2,1,0:T(8,128)(2,1)S(1)}, bf16[4,128,384]{2,1,0:T(8,128)(2,1)S(1)}, u32[]{:S(2)}, u32[]{:S(2)}) collective-permute-start(bf16[4,128,384]{2,1,0:T(8,128)(2,1)S(1)} %get-tuple-element.39), channel_id=1, source_target_pairs={{0,8},{8,0},{16,24},{24,16},{1,9},{9,1},{17,25},{25,17},{2,10},{10... | collective-permute-start | bytes 1179656 | tf_op jit(solution)/shard_map/ppermute | solution.py:25
  226.7 5.6 %collective-permute-done.35 = bf16[4,128,384]{2,1,0:T(8,128)(2,1)S(1)} collective-permute-done((bf16[4,128,384]{2,1,0:T(8,128)(2,1)S(1)}, bf16[4,128,384]{2,1,0:T(8,128)(2,1)S(1)}, u32[]{:S(2)}, u32[]{:S(2)}) %collective-permute-start.35) | collective-permute-done | bytes 393248 | tf_op jit(solution)/shard_map/ppermute | solution.py:25
  232.2 7.7 %collective-permute-start.27 = (bf16[1,192,768]{2,1,0:T(8,128)(2,1)S(1)}, bf16[1,192,768]{2,1,0:T(8,128)(2,1)S(1)}, u32[]{:S(2)}, u32[]{:S(2)}) collective-permute-start(bf16[1,192,768]{2,1,0:T(8,128)(2,1)S(1)} %get-tuple-element.48), channel_id=1, source_target_pairs={{0,3},{1,7},{2,2},{3,6},{4,1},{5,5},{6,0},{7,4},{8,11},{9,15},{10,... | collective-permute-start | bytes 884744 | tf_op jit(solution)/shard_map/ppermute | solution.py:25
  240.0 9.4 %collective-permute-done.38 = bf16[4,128,384]{2,1,0:T(8,128)(2,1)S(1)} collective-permute-done((bf16[4,128,384]{2,1,0:T(8,128)(2,1)S(1)}, bf16[4,128,384]{2,1,0:T(8,128)(2,1)S(1)}, u32[]{:S(2)}, u32[]{:S(2)}) %collective-permute-start.38) | collective-permute-done | bytes 393248 | tf_op jit(solution)/shard_map/ppermute | solution.py:25
  254.5 10.3 %collective-permute-start.49 = (bf16[3,192,384]{2,1,0:T(8,128)(2,1)S(1)}, bf16[3,192,384]{2,1,0:T(8,128)(2,1)S(1)}, u32[]{:S(2)}, u32[]{:S(2)}) collective-permute-start(bf16[3,192,384]{2,1,0:T(8,128)(2,1)S(1)} %get-tuple-element.32), channel_id=1, source_target_pairs={{0,3},{1,7},{2,2},{3,6},{4,1},{5,5},{6,0},{7,4},{8,11},{9,15},{10,... | collective-permute-start | bytes 1327112 | tf_op jit(solution)/shard_map/ppermute | solution.py:25
  269.3 7.9 %collective-permute-done.25 = bf16[1,192,768]{2,1,0:T(8,128)(2,1)S(1)} collective-permute-done((bf16[1,192,768]{2,1,0:T(8,128)(2,1)S(1)}, bf16[1,192,768]{2,1,0:T(8,128)(2,1)S(1)}, u32[]{:S(2)}, u32[]{:S(2)}) %collective-permute-start.25) | collective-permute-done | bytes 294944 | tf_op jit(solution)/shard_map/ppermute | solution.py:25
  277.8 7.3 %collective-permute-start.43 = (bf16[3,192,384]{2,1,0:T(8,128)(2,1)S(1)}, bf16[3,192,384]{2,1,0:T(8,128)(2,1)S(1)}, u32[]{:S(2)}, u32[]{:S(2)}) collective-permute-start(bf16[3,192,384]{2,1,0:T(8,128)(2,1)S(1)} %get-tuple-element.36), channel_id=1, source_target_pairs={{0,3},{1,7},{2,2},{3,6},{4,1},{5,5},{6,0},{7,4},{8,11},{9,15},{10,... | collective-permute-start | bytes 1327112 | tf_op jit(solution)/shard_map/ppermute | solution.py:25
  287.7 8.3 %collective-permute-done.43 = bf16[3,192,384]{2,1,0:T(8,128)(2,1)S(1)} collective-permute-done((bf16[3,192,384]{2,1,0:T(8,128)(2,1)S(1)}, bf16[3,192,384]{2,1,0:T(8,128)(2,1)S(1)}, u32[]{:S(2)}, u32[]{:S(2)}) %collective-permute-start.43) | collective-permute-done | bytes 442400 | tf_op jit(solution)/shard_map/ppermute | solution.py:25
  296.1 9.9 %collective-permute-done.42 = bf16[3,192,384]{2,1,0:T(8,128)(2,1)S(1)} collective-permute-done((bf16[3,192,384]{2,1,0:T(8,128)(2,1)S(1)}, bf16[3,192,384]{2,1,0:T(8,128)(2,1)S(1)}, u32[]{:S(2)}, u32[]{:S(2)}) %collective-permute-start.42) | collective-permute-done | bytes 442400 | tf_op jit(solution)/shard_map/ppermute | solution.py:25
  (228 shorter events, 108.1 us)
Async XLA Ops:
  0.6 22.9 %collective-permute-start.2 = (bf16[1,128,1536]{2,1,0:T(8,128)(2,1)}, bf16[1,128,1536]{2,1,0:T(8,128)(2,1)S(1)}, u32[]{:S(2)}, u32[]{:S(2)}) collective-permute-start(bf16[1,128,1536]{2,1,0:T(8,128)(2,1)} %param.6), channel_id=1, source_target_pairs={{0,8},{8,0},{16,24},{24,16},{1,9},{9,1},{17,25},{25,17},{2,10},{10... | collective-permute-start | bytes 1179656 | tf_op jit(solution)/shard_map/ppermute | solution.py:25
  3.7 39.6 %collective-permute-start.8 = (bf16[1,128,1536]{2,1,0:T(8,128)(2,1)}, bf16[1,128,1536]{2,1,0:T(8,128)(2,1)S(1)}, u32[]{:S(2)}, u32[]{:S(2)}) collective-permute-start(bf16[1,128,1536]{2,1,0:T(8,128)(2,1)} %param.6), channel_id=1, source_target_pairs={{8,16},{16,8},{9,17},{17,9},{10,18},{18,10},{11,19},{19,11},{12,20... | collective-permute-start | bytes 1179656 | tf_op jit(solution)/shard_map/ppermute | solution.py:25
  4.4 29.7 %collective-permute-start.5 = (bf16[1,128,1536]{2,1,0:T(8,128)(2,1)}, bf16[1,128,1536]{2,1,0:T(8,128)(2,1)S(1)}, u32[]{:S(2)}, u32[]{:S(2)}) collective-permute-start(bf16[1,128,1536]{2,1,0:T(8,128)(2,1)} %param.6), channel_id=1, source_target_pairs={{0,16},{8,24},{16,0},{24,8},{1,17},{9,25},{17,1},{25,9},{2,18},{10... | collective-permute-start | bytes 1179656 | tf_op jit(solution)/shard_map/ppermute | solution.py:25
  64.4 21.4 %collective-permute-start.13 = (bf16[4,128,384]{2,1,0:T(8,128)(2,1)}, bf16[4,128,384]{2,1,0:T(8,128)(2,1)}, u32[]{:S(2)}, u32[]{:S(2)}) collective-permute-start(bf16[4,128,384]{2,1,0:T(8,128)(2,1)} %pad_maximum_fusion.13), channel_id=1, source_target_pairs={{0,16},{8,24},{16,0},{24,8},{1,17},{9,25},{17,1},{25,9},{2,18},{10... | collective-permute-start | bytes 1179656 | tf_op jit(solution)/shard_map/ppermute | solution.py:25
  65.5 34.6 %collective-permute-start.12 = (bf16[4,128,384]{2,1,0:T(8,128)(2,1)}, bf16[4,128,384]{2,1,0:T(8,128)(2,1)}, u32[]{:S(2)}, u32[]{:S(2)}) collective-permute-start(bf16[4,128,384]{2,1,0:T(8,128)(2,1)} %pad_maximum_fusion.13), channel_id=1, source_target_pairs={{0,8},{8,0},{16,24},{24,16},{1,9},{9,1},{17,25},{25,17},{2,10},{10... | collective-permute-start | bytes 1179656 | tf_op jit(solution)/shard_map/ppermute | solution.py:25
  68.1 21.4 %collective-permute-start.14 = (bf16[4,128,384]{2,1,0:T(8,128)(2,1)}, bf16[4,128,384]{2,1,0:T(8,128)(2,1)}, u32[]{:S(2)}, u32[]{:S(2)}) collective-permute-start(bf16[4,128,384]{2,1,0:T(8,128)(2,1)} %pad_maximum_fusion.13), channel_id=1, source_target_pairs={{8,16},{16,8},{9,17},{17,9},{10,18},{18,10},{11,19},{19,11},{12,20... | collective-permute-start | bytes 1179656 | tf_op jit(solution)/shard_map/ppermute | solution.py:25
  114.7 18.7 %collective-permute-start.19 = (bf16[4,128,384]{2,1,0:T(8,128)(2,1)}, bf16[4,128,384]{2,1,0:T(8,128)(2,1)}, u32[]{:S(2)}, u32[]{:S(2)}) collective-permute-start(bf16[4,128,384]{2,1,0:T(8,128)(2,1)} %get-tuple-element.79), channel_id=1, source_target_pairs={{0,16},{8,24},{16,0},{24,8},{1,17},{9,25},{17,1},{25,9},{2,18},{10... | collective-permute-start | bytes 1179656 | tf_op jit(solution)/shard_map/ppermute | solution.py:25
  116.6 18.5 %collective-permute-start.20 = (bf16[4,128,384]{2,1,0:T(8,128)(2,1)}, bf16[4,128,384]{2,1,0:T(8,128)(2,1)S(1)}, u32[]{:S(2)}, u32[]{:S(2)}) collective-permute-start(bf16[4,128,384]{2,1,0:T(8,128)(2,1)} %get-tuple-element.79), channel_id=1, source_target_pairs={{8,16},{16,8},{9,17},{17,9},{10,18},{18,10},{11,19},{19,11},{12,20... | collective-permute-start | bytes 1179656 | tf_op jit(solution)/shard_map/ppermute | solution.py:25
  117.3 28.0 %collective-permute-start.18 = (bf16[4,128,384]{2,1,0:T(8,128)(2,1)}, bf16[4,128,384]{2,1,0:T(8,128)(2,1)S(1)}, u32[]{:S(2)}, u32[]{:S(2)}) collective-permute-start(bf16[4,128,384]{2,1,0:T(8,128)(2,1)} %get-tuple-element.79), channel_id=1, source_target_pairs={{0,8},{8,0},{16,24},{24,16},{1,9},{9,1},{17,25},{25,17},{2,10},{10... | collective-permute-start | bytes 1179656 | tf_op jit(solution)/shard_map/ppermute | solution.py:25
  173.2 46.0 %collective-permute-start.44 = (bf16[4,192,768]{2,1,0:T(8,128)(2,1)S(1)}, bf16[4,192,768]{2,1,0:T(8,128)(2,1)S(1)}, u32[]{:S(2)}, u32[]{:S(2)}) collective-permute-start(bf16[4,192,768]{2,1,0:T(8,128)(2,1)S(1)} %get-tuple-element.23), channel_id=1, source_target_pairs={{0,1},{1,0},{2,3},{3,2},{4,5},{5,4},{6,7},{7,6},{8,9},{9,8},{10,11... | collective-permute-start | bytes 3538952 | tf_op jit(solution)/shard_map/ppermute | solution.py:25
  174.1 40.7 %collective-permute-start.23 = (bf16[4,128,768]{2,1,0:T(8,128)(2,1)S(1)}, bf16[4,128,768]{2,1,0:T(8,128)(2,1)S(1)}, u32[]{:S(2)}, u32[]{:S(2)}) collective-permute-start(bf16[4,128,768]{2,1,0:T(8,128)(2,1)S(1)} %multiply_convert_fusion), channel_id=1, source_target_pairs={{0,1},{1,0},{2,3},{3,2},{4,5},{5,4},{6,7},{7,6},{8,9},{9,8},{10,11... | collective-permute-start | bytes 2359304 | tf_op jit(solution)/shard_map/ppermute | solution.py:25
  180.8 21.6 %collective-permute-start.32 = (bf16[4,128,384]{2,1,0:T(8,128)(2,1)S(1)}, bf16[4,128,384]{2,1,0:T(8,128)(2,1)S(1)}, u32[]{:S(2)}, u32[]{:S(2)}) collective-permute-start(bf16[4,128,384]{2,1,0:T(8,128)(2,1)S(1)} %add_convert_fusion.1), channel_id=1, source_target_pairs={{0,16},{8,24},{16,0},{24,8},{1,17},{9,25},{17,1},{25,9},{2,18},{10... | collective-permute-start | bytes 1179656 | tf_op jit(solution)/shard_map/ppermute | solution.py:25
  190.3 24.5 %collective-permute-start.22 = (bf16[4,128,768]{2,1,0:T(8,128)(2,1)S(1)}, bf16[4,128,768]{2,1,0:T(8,128)(2,1)S(1)}, u32[]{:S(2)}, u32[]{:S(2)}) collective-permute-start(bf16[4,128,768]{2,1,0:T(8,128)(2,1)S(1)} %get-tuple-element.44), channel_id=1, source_target_pairs={{0,1},{1,0},{2,3},{3,2},{4,5},{5,4},{6,7},{7,6},{8,9},{9,8},{10,11... | collective-permute-start | bytes 2359304 | tf_op jit(solution)/shard_map/ppermute | solution.py:25
  211.5 43.1 %collective-permute-start.28 = (bf16[4,192,768]{2,1,0:T(8,128)(2,1)S(1)}, bf16[4,192,768]{2,1,0:T(8,128)(2,1)S(1)}, u32[]{:S(2)}, u32[]{:S(2)}) collective-permute-start(bf16[4,192,768]{2,1,0:T(8,128)(2,1)S(1)} %get-tuple-element.25), channel_id=1, source_target_pairs={{0,1},{1,0},{2,3},{3,2},{4,5},{5,4},{6,7},{7,6},{8,9},{9,8},{10,11... | collective-permute-start | bytes 3538952 | tf_op jit(solution)/shard_map/ppermute | solution.py:25
  216.7 50.3 %collective-permute-start.24 = (bf16[1,192,768]{2,1,0:T(8,128)(2,1)S(1)}, bf16[1,192,768]{2,1,0:T(8,128)(2,1)S(1)}, u32[]{:S(2)}, u32[]{:S(2)}) collective-permute-start(bf16[1,192,768]{2,1,0:T(8,128)(2,1)S(1)} %get-tuple-element.47), channel_id=1, source_target_pairs={{0,0},{1,4},{2,1},{3,5},{4,2},{5,6},{6,3},{7,7},{8,8},{9,12},{10,9... | collective-permute-start | bytes 884744 | tf_op jit(solution)/shard_map/ppermute | solution.py:25
  218.2 21.7 %collective-permute-start.36 = (bf16[4,128,384]{2,1,0:T(8,128)(2,1)S(1)}, bf16[4,128,384]{2,1,0:T(8,128)(2,1)S(1)}, u32[]{:S(2)}, u32[]{:S(2)}) collective-permute-start(bf16[4,128,384]{2,1,0:T(8,128)(2,1)S(1)} %get-tuple-element.40), channel_id=1, source_target_pairs={{8,16},{16,8},{9,17},{17,9},{10,18},{18,10},{11,19},{19,11},{12,20... | collective-permute-start | bytes 1179656 | tf_op jit(solution)/shard_map/ppermute | solution.py:25
  223.8 25.6 %collective-permute-start.38 = (bf16[4,128,384]{2,1,0:T(8,128)(2,1)S(1)}, bf16[4,128,384]{2,1,0:T(8,128)(2,1)S(1)}, u32[]{:S(2)}, u32[]{:S(2)}) collective-permute-start(bf16[4,128,384]{2,1,0:T(8,128)(2,1)S(1)} %add_convert_fusion), channel_id=1, source_target_pairs={{0,16},{8,24},{16,0},{24,8},{1,17},{9,25},{17,1},{25,9},{2,18},{10... | collective-permute-start | bytes 1179656 | tf_op jit(solution)/shard_map/ppermute | solution.py:25
  232.2 35.8 %collective-permute-start.27 = (bf16[1,192,768]{2,1,0:T(8,128)(2,1)S(1)}, bf16[1,192,768]{2,1,0:T(8,128)(2,1)S(1)}, u32[]{:S(2)}, u32[]{:S(2)}) collective-permute-start(bf16[1,192,768]{2,1,0:T(8,128)(2,1)S(1)} %get-tuple-element.48), channel_id=1, source_target_pairs={{0,3},{1,7},{2,2},{3,6},{4,1},{5,5},{6,0},{7,4},{8,11},{9,15},{10,... | collective-permute-start | bytes 884744 | tf_op jit(solution)/shard_map/ppermute | solution.py:25
  239.9 28.2 %collective-permute-start.26 = (bf16[1,192,768]{2,1,0:T(8,128)(2,1)S(1)}, bf16[1,192,768]{2,1,0:T(8,128)(2,1)S(1)}, u32[]{:S(2)}, u32[]{:S(2)}) collective-permute-start(bf16[1,192,768]{2,1,0:T(8,128)(2,1)S(1)} %get-tuple-element.49), channel_id=1, source_target_pairs={{0,2},{1,6},{2,3},{3,7},{4,0},{5,4},{6,1},{7,5},{8,10},{9,14},{10,... | collective-permute-start | bytes 884744 | tf_op jit(solution)/shard_map/ppermute | solution.py:25
  253.8 24.1 %collective-permute-start.46 = (bf16[3,192,384]{2,1,0:T(8,128)(2,1)S(1)}, bf16[3,192,384]{2,1,0:T(8,128)(2,1)S(1)}, u32[]{:S(2)}, u32[]{:S(2)}) collective-permute-start(bf16[3,192,384]{2,1,0:T(8,128)(2,1)S(1)} %get-tuple-element.31), channel_id=1, source_target_pairs={{0,0},{1,4},{2,1},{3,5},{4,2},{5,6},{6,3},{7,7},{8,8},{9,12},{10,9... | collective-permute-start | bytes 1327112 | tf_op jit(solution)/shard_map/ppermute | solution.py:25
  254.5 30.6 %collective-permute-start.49 = (bf16[3,192,384]{2,1,0:T(8,128)(2,1)S(1)}, bf16[3,192,384]{2,1,0:T(8,128)(2,1)S(1)}, u32[]{:S(2)}, u32[]{:S(2)}) collective-permute-start(bf16[3,192,384]{2,1,0:T(8,128)(2,1)S(1)} %get-tuple-element.32), channel_id=1, source_target_pairs={{0,3},{1,7},{2,2},{3,6},{4,1},{5,5},{6,0},{7,4},{8,11},{9,15},{10,... | collective-permute-start | bytes 1327112 | tf_op jit(solution)/shard_map/ppermute | solution.py:25
  268.1 18.5 %collective-permute-start.47 = (bf16[3,192,384]{2,1,0:T(8,128)(2,1)S(1)}, bf16[3,192,384]{2,1,0:T(8,128)(2,1)S(1)}, u32[]{:S(2)}, u32[]{:S(2)}) collective-permute-start(bf16[3,192,384]{2,1,0:T(8,128)(2,1)S(1)} %get-tuple-element.34), channel_id=1, source_target_pairs={{0,1},{1,5},{2,0},{3,4},{4,3},{5,7},{6,2},{7,6},{8,9},{9,13},{10,8... | collective-permute-start | bytes 1327112 | tf_op jit(solution)/shard_map/ppermute | solution.py:25
  285.1 20.9 %collective-permute-start.42 = (bf16[3,192,384]{2,1,0:T(8,128)(2,1)S(1)}, bf16[3,192,384]{2,1,0:T(8,128)(2,1)S(1)}, u32[]{:S(2)}, u32[]{:S(2)}) collective-permute-start(bf16[3,192,384]{2,1,0:T(8,128)(2,1)S(1)} %get-tuple-element.37), channel_id=1, source_target_pairs={{0,2},{1,6},{2,3},{3,7},{4,0},{5,4},{6,1},{7,5},{8,10},{9,14},{10,... | collective-permute-start | bytes 1327112 | tf_op jit(solution)/shard_map/ppermute | solution.py:25
  285.2 20.8 %collective-permute-start.41 = (bf16[3,192,384]{2,1,0:T(8,128)(2,1)S(1)}, bf16[3,192,384]{2,1,0:T(8,128)(2,1)S(1)}, u32[]{:S(2)}, u32[]{:S(2)}) collective-permute-start(bf16[3,192,384]{2,1,0:T(8,128)(2,1)S(1)} %get-tuple-element.38), channel_id=1, source_target_pairs={{0,1},{1,5},{2,0},{3,4},{4,3},{5,7},{6,2},{7,6},{8,9},{9,13},{10,8... | collective-permute-start | bytes 1327112 | tf_op jit(solution)/shard_map/ppermute | solution.py:25
  (57 other events, 560.4 us)

commit v2 on v1

v2 whole, which is shorter than its diff:
```python
import jax
import jax.numpy as jnp
from jax import lax
from jax.sharding import PartitionSpec as P

DMAX = 32
F32 = jnp.float32
BF16 = jnp.bfloat16


def dot(spec, a, b):
    return jnp.einsum(spec, a, b, preferred_element_type=F32)


def activate(value):
    return jax.nn.gelu(value)


def activate_grad(pre, upstream):
    return jax.vjp(activate, pre)[1](upstream)[0]


def send(value, axis, pairs):
    return lax.ppermute(value, axis, pairs)


def swap(value, axis, mask):
    return send(value, axis, [(i, i ^ mask) for i in range(lax.axis_size(axis))])


def tied(*values):
    return lax.optimization_barrier(values)


def line_gather(block, beside=()):
    size = lax.axis_size("dp")
    if size != 4:
        blocks = [block] + [swap(block, "dp", m) for m in range(1, size)]
        return blocks[:-1], blocks[-1], beside
    far = swap(block, "dp", 2)
    near = swap(block, "dp", 1)
    far, near, beside = tied(far, near, beside)
    return [block, near, far], swap(far, "dp", 1), beside


def line_scatter(chunks, beside=()):
    size = lax.axis_size("dp")
    total = chunks[0].astype(F32)
    if size != 4:
        for m in range(1, size):
            total = total + swap(chunks[m], "dp", m).astype(F32)
        return total, beside
    passed = swap(chunks[3], "dp", 1)
    passed, first, beside = tied(passed, chunks[1], beside)
    far = swap((chunks[2].astype(F32) + passed.astype(F32)).astype(BF16), "dp", 2)
    near = swap(first, "dp", 1)
    return total + near.astype(F32) + far.astype(F32), beside


def exchange_edges(to_last, to_next):
    size = lax.axis_size("seq")
    first = lax.axis_index("seq") % 2 == 0
    inside = swap(jnp.where(first, to_next, to_last), "seq", 1)
    pairs = [(i, i + 1) for i in range(1, size - 1, 2)]
    outside = send(jnp.where(first, to_last, to_next), "seq", pairs + [(j, i) for i, j in pairs])
    return jnp.where(first, outside, inside), jnp.where(first, inside, outside)


def with_halo(value):
    length = value.shape[1]
    before, after = exchange_edges(value[:, :DMAX], value[:, length - DMAX :])
    return jnp.concatenate([before, value, after], axis=1)


def shifted_taps(padded, spacing, sign):
    length = padded.shape[1] - 2 * DMAX
    return [
        lax.dynamic_slice_in_dim(padded, DMAX + sign * (tap - 1) * spacing, length, 1)
        for tap in range(3)
    ]


def taps_sum(padded, weight, spacing, sign, spec):
    taps = shifted_taps(padded, spacing, sign)
    total = dot(spec, taps[0], weight[0])
    for tap in (1, 2):
        total = total + dot(spec, taps[tap], weight[tap])
    return total


def conv_edges(value, weight, spacing):
    length = value.shape[1]
    padded = jnp.pad(value, ((0, 0), (DMAX, DMAX), (0, 0)))
    to_next = lax.dynamic_slice_in_dim(padded, DMAX + length - spacing, DMAX, 1)
    to_last = lax.dynamic_slice_in_dim(padded, spacing, DMAX, 1)
    to_next = dot("blc,dc->bld", to_next, weight[0]).astype(BF16)
    to_last = dot("blc,dc->bld", to_last, weight[2]).astype(BF16)
    before, after = exchange_edges(to_last, to_next)
    total = taps_sum(padded, weight, spacing, 1, "blc,dc->bld")
    edges = jnp.pad(before, ((0, 0), (0, length - DMAX), (0, 0))).astype(F32)
    return total + edges + jnp.pad(after, ((0, 0), (length - DMAX, 0), (0, 0))).astype(F32)


def by_partner(value, dim):
    size = lax.axis_size("dp")
    width = value.shape[dim] // size
    place = lax.axis_index("dp")
    return jnp.concatenate(
        [lax.dynamic_slice_in_dim(value, (place ^ m) * width, width, dim) for m in range(size)],
        axis=dim,
    )


def chip_sum(parts, ordered):
    chips = lax.axis_size("seq") // 2
    core, layer = lax.axis_index("seq") % 2, lax.axis_index("dp")
    rows = parts[0].shape[0] // (2 * chips)
    width = parts[0].shape[0] // lax.axis_size("dp")

    def block(kind, chip):
        offset = (2 * chip + kind) * rows
        if ordered:
            offset = ((offset // width) ^ layer) * width + offset % width
        return jnp.stack([lax.dynamic_slice_in_dim(part, offset, rows, 0) for part in parts])

    given = jnp.stack([block(1 - core, chip) for chip in range(chips)])
    kept = jnp.stack([block(core, chip) for chip in range(chips)])
    return (kept.astype(F32) + swap(given, "seq", 1).astype(F32)).astype(BF16)


def chip_blocks(blocks):
    chip = lax.axis_index("seq") // 2
    return [lax.dynamic_index_in_dim(blocks, chip ^ j, 0, False) for j in range(blocks.shape[0])]


def spread(chosen, steps):
    return [swap(chosen[j], "seq", 2 * j) for j in steps]


def total_of(parts):
    return sum(part.astype(F32) for part in parts)


def channel_blocks(value, ordered):
    chips, chip = lax.axis_size("seq") // 2, lax.axis_index("seq") // 2
    wide = value.shape[2] // chips
    width = value.shape[2] // lax.axis_size("dp")
    received = []
    for j in range(chips):
        offset = (chip ^ j) * wide
        if ordered:
            offset = ((offset // width) ^ lax.axis_index("dp")) * width + offset % width
        block = lax.dynamic_slice_in_dim(value, offset, wide, 2)
        received.append(swap(block, "seq", 2 * j) if j else block)
    return received


def bin_blocks(value):
    chips = lax.axis_size("seq") // 2
    return [value] + [swap(value, "seq", 2 * j) for j in range(1, chips)]


def core_sum(parts):
    stacked = jnp.stack(parts)
    rows = stacked.shape[1] // 2
    core = lax.axis_index("seq") % 2
    kept = lax.dynamic_slice_in_dim(stacked, core * rows, rows, 1)
    given = lax.dynamic_slice_in_dim(stacked, (1 - core) * rows, rows, 1).astype(BF16)
    return kept + swap(given, "seq", 1).astype(F32)


def weight_parts(taps, upstream):
    return [dot("blc,bld->cd", *pair) for pair in zip(taps, upstream)]


def on_device(embeddings, conv_one, conv_two, head_weight, counts, dilation):
    length = embeddings.shape[1]
    size = lax.axis_size("dp")
    width = conv_one.shape[1]
    batch = counts.shape[0]
    layer = lax.axis_index("dp")
    first_gap, second_gap = dilation[0], dilation[1]
    all_bins = length * lax.axis_size("seq")
    per_layer = embeddings.shape[0]

    def absolute(value):
        stacked = value.reshape((size, per_layer) + value.shape[1:])
        picked = [lax.dynamic_index_in_dim(stacked, layer ^ b, 0, False) for b in range(size)]
        return jnp.concatenate(picked, axis=0)

    def layer_one(blocks):
        value = jnp.concatenate(blocks, axis=0)
        frame = with_halo(value)
        pre = taps_sum(frame, conv_one, first_gap, 1, "blc,dc->bld")
        own = lax.dynamic_slice_in_dim(value, layer * width, width, 2)
        return frame, pre, (own.astype(F32) + activate(pre)).astype(BF16)

    early, late, _ = line_gather(embeddings)
    made = [layer_one(early), layer_one([late])]
    framed_in, pre_one, hidden_one = [jnp.concatenate(some, axis=0) for some in zip(*made)]
    pre_one, hidden_one = absolute(pre_one), absolute(hidden_one)

    conv_two_r = by_partner(conv_two, 2)
    head_r = by_partner(head_weight, 0)
    targets = counts.astype(F32)

    hidden_one, framed_in = tied(hidden_one, framed_in)
    in_blocks = channel_blocks(framed_in, False)
    early, late, _ = line_gather(hidden_one)
    rows_one = jnp.concatenate(early + [late], axis=2)
    rows_one, in_blocks[:-1] = tied(rows_one, in_blocks[:-1])
    pre_two = conv_edges(rows_one, conv_two_r, second_gap)
    hidden_two = (hidden_one.astype(F32) + activate(pre_two)).astype(BF16)

    hidden_two, rows_one, in_blocks[-1] = tied(hidden_two, rows_one, in_blocks[-1])
    one_blocks = channel_blocks(rows_one, True)
    early, late, _ = line_gather(hidden_two)
    rows_two = jnp.concatenate(early + [late], axis=2)
    rows_two, one_blocks[:-1] = tied(rows_two, one_blocks[:-1])
    logits = dot("blc,ct->blt", rows_two, head_r)
    peak = jnp.max(logits, axis=1)
    total = jnp.sum(jnp.exp(logits - peak[:, None, :]), axis=1)
    cross = jnp.sum(targets * logits, axis=1)
    every = lax.all_gather(jnp.stack([peak, total, jnp.sum(targets, axis=1), cross]), "seq")
    every, one_blocks[-1] = tied(every, one_blocks[-1])
    one_blocks, in_blocks = jnp.concatenate(one_blocks, axis=0), jnp.concatenate(in_blocks, axis=0)
    peak = jnp.max(every[:, 0], axis=0)
    total = jnp.sum(every[:, 1] * jnp.exp(every[:, 0] - peak), axis=0)
    count_total = jnp.sum(every[:, 2], axis=0)
    cross_total = jnp.sum(every[:, 3], axis=0)
    log_total = peak + jnp.log(total)
    track_loss = (count_total * log_total - cross_total) / all_bins
    logit_grad = (
        (count_total[:, None] * jnp.exp(logits - log_total[:, None]) - targets) / all_bins
    ).astype(BF16)

    back = dot("blt,ct->blc", logit_grad, head_r).astype(BF16)
    logit_grad, back = tied(logit_grad, back)
    head_part = dot("blc,blt->ct", rows_two, logit_grad).astype(BF16)
    head_blocks = chip_blocks(chip_sum([head_part], True))
    near_steps, far_steps = range(1, len(head_blocks) - 1), range(len(head_blocks) - 1, len(head_blocks))
    head_near, head_far = spread(head_blocks, near_steps), spread(head_blocks, far_steps)
    grad_two_out, _ = line_scatter(jnp.split(back, size, axis=2))
    up_two = activate_grad(pre_two, grad_two_out).astype(BF16)
    up_two, head_near = tied(up_two, head_near)

    framed_back = with_halo(up_two)
    back = taps_sum(framed_back, conv_two_r, second_gap, -1, "bld,dc->blc").astype(BF16)
    framed_back, back, head_far = tied(framed_back, back, head_far)
    grad_head = total_of(head_blocks[:1] + head_near + head_far)[0]
    back_blocks = bin_blocks(framed_back)
    summed, back_blocks[:-1] = line_scatter(jnp.split(back, size, axis=2), back_blocks[:-1])
    summed, back_blocks[-1] = tied(summed, back_blocks[-1])
    up_taps = shifted_taps(jnp.concatenate(back_blocks, axis=0), second_gap, -1)
    grad_two = core_sum(weight_parts([one_blocks] * 3, up_taps))

    up_one = absolute(activate_grad(pre_one, grad_two_out + summed).astype(BF16))
    up_blocks = bin_blocks(up_one)
    up_all = jnp.concatenate(up_blocks, axis=0)
    grad_one = core_sum(weight_parts(shifted_taps(in_blocks, first_gap, 1), [up_all] * 3))
    return (track_loss, grad_head, grad_one, grad_two)


def solution(mesh):
    placed = (
        P("dp", "seq", None),
        P(None, "dp", None),
        P(None, "dp", None),
        P(None, "dp"),
        P(None, "seq", "dp"),
        P(),
    )
    return jax.shard_map(
        on_device,
        mesh=mesh,
        in_specs=placed,
        out_specs=(P(None, "dp"), P("seq", "dp"), P(None, "seq", "dp"), P(None, "seq", "dp")),
        check_vma=False,
    )
```

time: 308 us -> 262 us (0.85)
  waiting for transfers between devices: 134 us -> 111 us
  starting transfers between devices: 91.8 us -> 74 us
  matrix products: 33.2 us -> 25.2 us
  blocking collectives: 18.4 us -> 11 us
  local copies, waits for them, and re-layouts: 9.01 us -> 15.7 us
    ppermute x50 -> x41, waiting for transfers between devices: 134 us -> 111 us  [send(): return lax.ppermute(value, axis, pairs)]
    ppermute x50 -> x41, starting transfers between devices: 91.8 us -> 74 us  [send(): return lax.ppermute(value, axis, pairs)]
    dot_general x27 -> x23, matrix products: 33.2 us -> 25.2 us  [dot(): return jnp.einsum(spec, a, b, preferred_element_type=F32)]
    all_gather x1, blocking collectives: 18.4 us -> 11 us  [on_device(): lax.all_gather(jnp.stack([peak, total, jnp.sum(targets, axis=1), cross]),...]
  transfers between devices with their start and end apart: 50 -> 41, of which waited for: 19 -> 19; matrix products, arithmetic and copies ran while one was open for 12% -> 17% of each run, Pallas kernels for 0% -> 0%
where the time goes in v2:
time: 262 us
  waiting for transfers between devices  111 us (42%)
  starting transfers between devices  74 us (28%)
  matrix products  25.2 us (10%)
  other arithmetic  16.3 us (6%)
  local copies, waits for them, and re-layouts  15.7 us (6%)
  blocking collectives  11 us (4%)
  between operations  8.66 us (3%)
    ppermute x41, waiting for transfers between devices, send(): return lax.ppermute(value, axis, pairs)  111 us
    ppermute x41, starting transfers between devices, send(): return lax.ppermute(value, axis, pairs)  74 us
    dot_general x23, matrix products, dot(): return jnp.einsum(spec, a, b, preferred_element_type=F32)  25.2 us
    all_gather x1, blocking collectives, on_device(): lax.all_gather(jnp.stack([peak, total, jnp.sum(targets, axis=1), cross]),...  11 us
  transfers between devices with their start and end apart: 41, of which 19 were waited for; matrix products, arithmetic and copies ran while one was open for 17% of the time, Pallas kernels for 0%

profile of v2, /device:TPU:0, one launch (start us, length us, event | category | flops | bytes accessed | tf_op | source)
XLA Modules:
  0.0 261.6 jit_solution(15196500184343074568)
XLA Ops:
  0.6 4.1 %collective-permute-start = (bf16[1,128,1536]{2,1,0:T(8,128)(2,1)}, bf16[1,128,1536]{2,1,0:T(8,128)(2,1)S(1)}, u32[]{:S(2)}, u32[]{:S(2)}) collective-permute-start(bf16[1,128,1536]{2,1,0:T(8,128)(2,1)} %param.6), channel_id=1, source_target_pairs={{0,16},{8,24},{16,0},{24,8},{1,17},{9,25},{17,1},{25,9},{2,18},{10... | collective-permute-start | bytes 1179656 | tf_op jit(solution)/shard_map/ppermute | solution.py:24
  10.8 11.8 %collective-permute-done = bf16[1,128,1536]{2,1,0:T(8,128)(2,1)S(1)} collective-permute-done((bf16[1,128,1536]{2,1,0:T(8,128)(2,1)}, bf16[1,128,1536]{2,1,0:T(8,128)(2,1)S(1)}, u32[]{:S(2)}, u32[]{:S(2)}) %collective-permute-start) | collective-permute-done | bytes 393248 | tf_op jit(solution)/shard_map/ppermute | solution.py:24
  25.1 2.9 %collective-permute-start.3 = (bf16[3,32,1536]{2,1,0:T(8,128)(2,1)S(1)}, bf16[3,32,1536]{2,1,0:T(8,128)(2,1)S(1)}, u32[]{:S(2)}, u32[]{:S(2)}) collective-permute-start(bf16[3,32,1536]{2,1,0:T(8,128)(2,1)S(1)} %get-tuple-element.127), channel_id=1, source_target_pairs={{0,1},{1,0},{2,3},{3,2},{4,5},{5,4},{6,7},{7,6},{8,9},{9,8},{10,11... | collective-permute-start | bytes 884744 | tf_op jit(solution)/shard_map/ppermute | solution.py:24
  30.2 2.7 %collective-permute-done.4 = bf16[1,128,1536]{2,1,0:T(8,128)(2,1)S(1)} collective-permute-done((bf16[1,128,1536]{2,1,0:T(8,128)(2,1)S(1)}, bf16[1,128,1536]{2,1,0:T(8,128)(2,1)S(1)}, u32[]{:S(2)}, u32[]{:S(2)}) %collective-permute-start.4) | collective-permute-done | bytes 393248 | tf_op jit(solution)/shard_map/ppermute | solution.py:24
  33.5 4.1 %collective-permute-start.6 = (bf16[1,32,1536]{2,1,0:T(8,128)(2,1)S(1)}, bf16[1,32,1536]{2,1,0:T(8,128)(2,1)S(1)}, u32[]{:S(2)}, u32[]{:S(2)}) collective-permute-start(bf16[1,32,1536]{2,1,0:T(8,128)(2,1)S(1)} %get-tuple-element.141), channel_id=1, source_target_pairs={{0,1},{1,0},{2,3},{3,2},{4,5},{5,4},{6,7},{7,6},{8,9},{9,8},{10,11... | collective-permute-start | bytes 294920 | tf_op jit(solution)/shard_map/ppermute | solution.py:24
  43.6 3.0 %collective-permute-start.7 = (bf16[4,128,384]{2,1,0:T(8,128)(2,1)}, bf16[4,128,384]{2,1,0:T(8,128)(2,1)}, u32[]{:S(2)}, u32[]{:S(2)}) collective-permute-start(bf16[4,128,384]{2,1,0:T(8,128)(2,1)} %pad_maximum_fusion.10), channel_id=1, source_target_pairs={{0,16},{8,24},{16,0},{24,8},{1,17},{9,25},{17,1},{25,9},{2,18},{10... | collective-permute-start | bytes 1179656 | tf_op jit(solution)/shard_map/ppermute | solution.py:24
  55.4 4.4 %collective-permute-start.11 = (bf16[4,192,384]{2,1,0:T(8,128)(2,1)S(1)}, bf16[4,192,384]{2,1,0:T(8,128)(2,1)S(1)}, u32[]{:S(2)}, u32[]{:S(2)}) collective-permute-start(bf16[4,192,384]{2,1,0:T(8,128)(2,1)S(1)} %get-tuple-element.112), channel_id=1, source_target_pairs={{0,4},{1,5},{2,6},{3,7},{4,0},{5,1},{6,2},{7,3},{8,12},{9,13},{10,... | collective-permute-start | bytes 1769480 | tf_op jit(solution)/shard_map/ppermute | solution.py:24
  65.3 4.1 %collective-permute-start.14 = (bf16[4,192,384]{2,1,0:T(8,128)(2,1)S(1)}, bf16[4,192,384]{2,1,0:T(8,128)(2,1)}, u32[]{:S(2)}, u32[]{:S(2)}) collective-permute-start(bf16[4,192,384]{2,1,0:T(8,128)(2,1)S(1)} %get-tuple-element.111), channel_id=1, source_target_pairs={{0,6},{1,7},{2,4},{3,5},{4,2},{5,3},{6,0},{7,1},{8,14},{9,15},{10,... | collective-permute-start | bytes 1769480 | tf_op jit(solution)/shard_map/ppermute | solution.py:24
  69.4 5.4 %collective-permute-done.9 = bf16[4,128,384]{2,1,0:T(8,128)(2,1)S(1)} collective-permute-done((bf16[4,128,384]{2,1,0:T(8,128)(2,1)}, bf16[4,128,384]{2,1,0:T(8,128)(2,1)S(1)}, u32[]{:S(2)}, u32[]{:S(2)}) %collective-permute-start.9) | collective-permute-done | bytes 393248 | tf_op jit(solution)/shard_map/ppermute | solution.py:24
  79.2 6.2 %collective-permute-start.13 = (bf16[4,32,384]{2,1,0:T(8,128)(2,1)S(1)}, bf16[4,32,384]{2,1,0:T(8,128)(2,1)S(1)}, u32[]{:S(2)}, u32[]{:S(2)}) collective-permute-start(bf16[4,32,384]{2,1,0:T(8,128)(2,1)S(1)} %get-tuple-element.147), channel_id=1, source_target_pairs={{0,1},{1,0},{2,3},{3,2},{4,5},{5,4},{6,7},{7,6},{8,9},{9,8},{10,11... | collective-permute-start | bytes 294920 | tf_op jit(solution)/shard_map/ppermute | solution.py:24
  86.4 3.2 %add_convert_fusion.3 = (bf16[4,128,384]{2,1,0:T(8,128)(2,1)S(1)}, f32[4,128,384]{2,1,0:T(8,128)}) fusion(bf16[4,128,384]{2,1,0:T(8,128)(2,1)} %pad_maximum_fusion.10, bf16[4,32,384]{2,1,0:T(8,128)(2,1)S(1)} %get-tuple-element.145, bf16[4,32,384]{2,1,0:T(8,128)(2,1)S(1)} %get-tuple-element.144, f32[4,128,384]{2,1,0:T(8,128)S(1)} %fusion.2, ...), kind=kOutput, calls=%fused_computation.114 | convolution fusion | flops 607322112 | bytes 6094852 | tf_op jit(solution)/shard_map/blc,dc->bld/dot_general | solution.py:12
  91.0 3.3 %collective-permute-start.15 = (bf16[4,128,384]{2,1,0:T(8,128)(2,1)S(1)}, bf16[4,128,384]{2,1,0:T(8,128)(2,1)}, u32[]{:S(2)}, u32[]{:S(2)}) collective-permute-start(bf16[4,128,384]{2,1,0:T(8,128)(2,1)S(1)} %get-tuple-element.49), channel_id=1, source_target_pairs={{0,16},{8,24},{16,0},{24,8},{1,17},{9,25},{17,1},{25,9},{2,18},{10... | collective-permute-start | bytes 1179656 | tf_op jit(solution)/shard_map/ppermute | solution.py:24
  94.3 14.4 %collective-permute-done.16 = bf16[4,128,384]{2,1,0:T(8,128)(2,1)S(1)} collective-permute-done((bf16[4,128,384]{2,1,0:T(8,128)(2,1)S(1)}, bf16[4,128,384]{2,1,0:T(8,128)(2,1)S(1)}, u32[]{:S(2)}, u32[]{:S(2)}) %collective-permute-start.16) | collective-permute-done | bytes 393248 | tf_op jit(solution)/shard_map/ppermute | solution.py:24
  109.4 3.2 %collective-permute-start.17 = (bf16[4,128,384]{2,1,0:T(8,128)(2,1)}, bf16[4,128,384]{2,1,0:T(8,128)(2,1)}, u32[]{:S(2)}, u32[]{:S(2)}) collective-permute-start(bf16[4,128,384]{2,1,0:T(8,128)(2,1)} %collective-permute-done.15), channel_id=1, source_target_pairs={{0,8},{8,0},{16,24},{24,16},{1,9},{9,1},{17,25},{25,17},{2,10},{10... | collective-permute-start | bytes 1179656 | tf_op jit(solution)/shard_map/ppermute | solution.py:24
  112.6 3.1 %constant_dynamic-slice_fusion.4 = (bf16[4,128,384]{2,1,0:T(8,128)(2,1)S(1)}, bf16[4,128,384]{2,1,0:T(8,128)(2,1)S(1)}, bf16[4,128,384]{2,1,0:T(8,128)(2,1)S(1)}, bf16[4,128,384]{2,1,0:T(8,128)(2,1)}) fusion(bf16[4,128,1536]{2,1,0:T(8,128)(2,1)} %copy-done, s32[]{:T(128)S(6)} %select_n.366, s32[]{:T(128)S(6)} %select_n.363, s32[]{:T(128)S(6)} %select_n.360, ...), kind=kLoop, calls=%fused_computation.233 | loop fusion | bytes 3145744 | tf_op jit(solution)/shard_map/dynamic_slice | solution.py:153
  123.2 3.7 %collective-permute-done.19 = bf16[4,128,384]{2,1,0:T(8,128)(2,1)S(1)} collective-permute-done((bf16[4,128,384]{2,1,0:T(8,128)(2,1)S(1)}, bf16[4,128,384]{2,1,0:T(8,128)(2,1)S(1)}, u32[]{:S(2)}, u32[]{:S(2)}) %collective-permute-start.19) | collective-permute-done | bytes 393248 | tf_op jit(solution)/shard_map/ppermute | solution.py:24
  131.7 11.0 %all-gather = f32[32,4,768]{2,1,0:T(4,128)S(1)} all-gather(f32[4,4,768]{2,1,0:T(4,128)S(1)} %pad_maximum_fusion.12), channel_id=2, replica_groups=mesh['dp'=4,'seq'=8] {'seq'}, dimensions={0}, use_global_device_ids=true | all-gather | bytes 442368 | tf_op jit(solution)/shard_map/all_gather | solution.py:224
  153.9 8.4 %collective-permute-done.22 = bf16[4,128,384]{2,1,0:T(8,128)(2,1)} collective-permute-done((bf16[4,128,384]{2,1,0:T(8,128)(2,1)}, bf16[4,128,384]{2,1,0:T(8,128)(2,1)}, u32[]{:S(2)}, u32[]{:S(2)}) %collective-permute-start.22) | collective-permute-done | bytes 393248 | tf_op jit(solution)/shard_map/ppermute | solution.py:24
  163.4 3.5 %collective-permute-start.24 = (bf16[4,128,384]{2,1,0:T(8,128)(2,1)S(1)}, bf16[4,128,384]{2,1,0:T(8,128)(2,1)S(1)}, u32[]{:S(2)}, u32[]{:S(2)}) collective-permute-start(bf16[4,128,384]{2,1,0:T(8,128)(2,1)S(1)} %add_convert_fusion.2), channel_id=1, source_target_pairs={{0,16},{8,24},{16,0},{24,8},{1,17},{9,25},{17,1},{25,9},{2,18},{10... | collective-permute-start | bytes 1179656 | tf_op jit(solution)/shard_map/ppermute | solution.py:24
  171.1 12.9 %collective-permute-done.24 = bf16[4,128,384]{2,1,0:T(8,128)(2,1)S(1)} collective-permute-done((bf16[4,128,384]{2,1,0:T(8,128)(2,1)S(1)}, bf16[4,128,384]{2,1,0:T(8,128)(2,1)S(1)}, u32[]{:S(2)}, u32[]{:S(2)}) %collective-permute-start.24) | collective-permute-done | bytes 393248 | tf_op jit(solution)/shard_map/ppermute | solution.py:24
  194.5 3.7 %collective-permute-start.32 = (bf16[4,192,384]{2,1,0:T(8,128)(2,1)S(1)}, bf16[4,192,384]{2,1,0:T(8,128)(2,1)S(1)}, u32[]{:S(2)}, u32[]{:S(2)}) collective-permute-start(bf16[4,192,384]{2,1,0:T(8,128)(2,1)S(1)} %pad_maximum_fusion.9), channel_id=1, source_target_pairs={{0,4},{1,5},{2,6},{3,7},{4,0},{5,1},{6,2},{7,3},{8,12},{9,13},{10,... | collective-permute-start | bytes 1769480 | tf_op jit(solution)/shard_map/ppermute | solution.py:24
  200.8 9.4 %collective-permute-done.30 = bf16[4,128,384]{2,1,0:T(8,128)(2,1)S(1)} collective-permute-done((bf16[4,128,384]{2,1,0:T(8,128)(2,1)S(1)}, bf16[4,128,384]{2,1,0:T(8,128)(2,1)S(1)}, u32[]{:S(2)}, u32[]{:S(2)}) %collective-permute-start.30) | collective-permute-done | bytes 393248 | tf_op jit(solution)/shard_map/ppermute | solution.py:24
  217.0 15.9 %collective-permute-done.34 = bf16[4,128,384]{2,1,0:T(8,128)(2,1)S(1)} collective-permute-done((bf16[4,128,384]{2,1,0:T(8,128)(2,1)S(1)}, bf16[4,128,384]{2,1,0:T(8,128)(2,1)S(1)}, u32[]{:S(2)}, u32[]{:S(2)}) %collective-permute-start.34) | collective-permute-done | bytes 393248 | tf_op jit(solution)/shard_map/ppermute | solution.py:24
  241.0 14.0 %collective-permute-done.36 = bf16[4,128,384]{2,1,0:T(8,128)(2,1)S(1)} collective-permute-done((bf16[4,128,384]{2,1,0:T(8,128)(2,1)S(1)}, bf16[4,128,384]{2,1,0:T(8,128)(2,1)S(1)}, u32[]{:S(2)}, u32[]{:S(2)}) %collective-permute-start.36) | collective-permute-done | bytes 393248 | tf_op jit(solution)/shard_map/ppermute | solution.py:24
  (212 shorter events, 94.6 us)
Async XLA Ops:
  0.6 22.0 %collective-permute-start = (bf16[1,128,1536]{2,1,0:T(8,128)(2,1)}, bf16[1,128,1536]{2,1,0:T(8,128)(2,1)S(1)}, u32[]{:S(2)}, u32[]{:S(2)}) collective-permute-start(bf16[1,128,1536]{2,1,0:T(8,128)(2,1)} %param.6), channel_id=1, source_target_pairs={{0,16},{8,24},{16,0},{24,8},{1,17},{9,25},{17,1},{25,9},{2,18},{10... | collective-permute-start | bytes 1179656 | tf_op jit(solution)/shard_map/ppermute | solution.py:24
  4.7 18.0 %collective-permute-start.1 = (bf16[1,128,1536]{2,1,0:T(8,128)(2,1)}, bf16[1,128,1536]{2,1,0:T(8,128)(2,1)S(1)}, u32[]{:S(2)}, u32[]{:S(2)}) collective-permute-start(bf16[1,128,1536]{2,1,0:T(8,128)(2,1)} %param.6), channel_id=1, source_target_pairs={{0,8},{8,0},{16,24},{24,16},{1,9},{9,1},{17,25},{25,17},{2,10},{10... | collective-permute-start | bytes 1179656 | tf_op jit(solution)/shard_map/ppermute | solution.py:24
  43.0 19.5 %collective-permute-start.8 = (bf16[4,128,384]{2,1,0:T(8,128)(2,1)}, bf16[4,128,384]{2,1,0:T(8,128)(2,1)S(1)}, u32[]{:S(2)}, u32[]{:S(2)}) collective-permute-start(bf16[4,128,384]{2,1,0:T(8,128)(2,1)} %pad_maximum_fusion.10), channel_id=1, source_target_pairs={{0,8},{8,0},{16,24},{24,16},{1,9},{9,1},{17,25},{25,17},{2,10},{10... | collective-permute-start | bytes 1179656 | tf_op jit(solution)/shard_map/ppermute | solution.py:24
  43.6 18.9 %collective-permute-start.7 = (bf16[4,128,384]{2,1,0:T(8,128)(2,1)}, bf16[4,128,384]{2,1,0:T(8,128)(2,1)}, u32[]{:S(2)}, u32[]{:S(2)}) collective-permute-start(bf16[4,128,384]{2,1,0:T(8,128)(2,1)} %pad_maximum_fusion.10), channel_id=1, source_target_pairs={{0,16},{8,24},{16,0},{24,8},{1,17},{9,25},{17,1},{25,9},{2,18},{10... | collective-permute-start | bytes 1179656 | tf_op jit(solution)/shard_map/ppermute | solution.py:24
  55.4 20.7 %collective-permute-start.11 = (bf16[4,192,384]{2,1,0:T(8,128)(2,1)S(1)}, bf16[4,192,384]{2,1,0:T(8,128)(2,1)S(1)}, u32[]{:S(2)}, u32[]{:S(2)}) collective-permute-start(bf16[4,192,384]{2,1,0:T(8,128)(2,1)S(1)} %get-tuple-element.112), channel_id=1, source_target_pairs={{0,4},{1,5},{2,6},{3,7},{4,0},{5,1},{6,2},{7,3},{8,12},{9,13},{10,... | collective-permute-start | bytes 1769480 | tf_op jit(solution)/shard_map/ppermute | solution.py:24
  59.8 16.3 %collective-permute-start.10 = (bf16[4,192,384]{2,1,0:T(8,128)(2,1)S(1)}, bf16[4,192,384]{2,1,0:T(8,128)(2,1)S(1)}, u32[]{:S(2)}, u32[]{:S(2)}) collective-permute-start(bf16[4,192,384]{2,1,0:T(8,128)(2,1)S(1)} %get-tuple-element.113), channel_id=1, source_target_pairs={{0,2},{1,3},{2,0},{3,1},{4,6},{5,7},{6,4},{7,5},{8,10},{9,11},{10,... | collective-permute-start | bytes 1769480 | tf_op jit(solution)/shard_map/ppermute | solution.py:24
  65.3 24.3 %collective-permute-start.14 = (bf16[4,192,384]{2,1,0:T(8,128)(2,1)S(1)}, bf16[4,192,384]{2,1,0:T(8,128)(2,1)}, u32[]{:S(2)}, u32[]{:S(2)}) collective-permute-start(bf16[4,192,384]{2,1,0:T(8,128)(2,1)S(1)} %get-tuple-element.111), channel_id=1, source_target_pairs={{0,6},{1,7},{2,4},{3,5},{4,2},{5,3},{6,0},{7,1},{8,14},{9,15},{10,... | collective-permute-start | bytes 1769480 | tf_op jit(solution)/shard_map/ppermute | solution.py:24
  89.6 19.1 %collective-permute-start.16 = (bf16[4,128,384]{2,1,0:T(8,128)(2,1)S(1)}, bf16[4,128,384]{2,1,0:T(8,128)(2,1)S(1)}, u32[]{:S(2)}, u32[]{:S(2)}) collective-permute-start(bf16[4,128,384]{2,1,0:T(8,128)(2,1)S(1)} %get-tuple-element.49), channel_id=1, source_target_pairs={{0,8},{8,0},{16,24},{24,16},{1,9},{9,1},{17,25},{25,17},{2,10},{10... | collective-permute-start | bytes 1179656 | tf_op jit(solution)/shard_map/ppermute | solution.py:24
  91.0 17.7 %collective-permute-start.15 = (bf16[4,128,384]{2,1,0:T(8,128)(2,1)S(1)}, bf16[4,128,384]{2,1,0:T(8,128)(2,1)}, u32[]{:S(2)}, u32[]{:S(2)}) collective-permute-start(bf16[4,128,384]{2,1,0:T(8,128)(2,1)S(1)} %get-tuple-element.49), channel_id=1, source_target_pairs={{0,16},{8,24},{16,0},{24,8},{1,17},{9,25},{17,1},{25,9},{2,18},{10... | collective-permute-start | bytes 1179656 | tf_op jit(solution)/shard_map/ppermute | solution.py:24
  119.0 23.7 %collective-permute-start.20 = (bf16[4,128,384]{2,1,0:T(8,128)(2,1)S(1)}, bf16[4,128,384]{2,1,0:T(8,128)(2,1)S(1)}, u32[]{:S(2)}, u32[]{:S(2)}) collective-permute-start(bf16[4,128,384]{2,1,0:T(8,128)(2,1)S(1)} %get-tuple-element.119), channel_id=1, source_target_pairs={{0,6},{1,7},{2,4},{3,5},{4,2},{5,3},{6,0},{7,1},{8,14},{9,15},{10,... | collective-permute-start | bytes 1179656 | tf_op jit(solution)/shard_map/ppermute | solution.py:24
  149.4 17.8 %collective-permute-start.21 = (bf16[4,1,192,768]{3,2,1,0:T(8,128)(2,1)}, bf16[4,1,192,768]{3,2,1,0:T(8,128)(2,1)}, u32[]{:S(2)}, u32[]{:S(2)}) collective-permute-start(bf16[4,1,192,768]{3,2,1,0:T(8,128)(2,1)} %pad_maximum_fusion.6), channel_id=1, source_target_pairs={{0,1},{1,0},{2,3},{3,2},{4,5},{5,4},{6,7},{7,6},{8,9},{9,8},{10,11... | collective-permute-start | bytes 3538952 | tf_op jit(solution)/shard_map/ppermute | solution.py:24
  163.4 20.7 %collective-permute-start.24 = (bf16[4,128,384]{2,1,0:T(8,128)(2,1)S(1)}, bf16[4,128,384]{2,1,0:T(8,128)(2,1)S(1)}, u32[]{:S(2)}, u32[]{:S(2)}) collective-permute-start(bf16[4,128,384]{2,1,0:T(8,128)(2,1)S(1)} %add_convert_fusion.2), channel_id=1, source_target_pairs={{0,16},{8,24},{16,0},{24,8},{1,17},{9,25},{17,1},{25,9},{2,18},{10... | collective-permute-start | bytes 1179656 | tf_op jit(solution)/shard_map/ppermute | solution.py:24
  166.9 18.4 %collective-permute-start.23 = (bf16[4,128,384]{2,1,0:T(8,128)(2,1)S(1)}, bf16[4,128,384]{2,1,0:T(8,128)(2,1)S(1)}, u32[]{:S(2)}, u32[]{:S(2)}) collective-permute-start(bf16[4,128,384]{2,1,0:T(8,128)(2,1)S(1)} %copy-done.28), channel_id=1, source_target_pairs={{0,8},{8,0},{16,24},{24,16},{1,9},{9,1},{17,25},{25,17},{2,10},{10... | collective-permute-start | bytes 1179656 | tf_op jit(solution)/shard_map/ppermute | solution.py:24
  168.9 18.5 %collective-permute-start.26 = (bf16[1,192,768]{2,1,0:T(8,128)(2,1)S(1)}, bf16[1,192,768]{2,1,0:T(8,128)(2,1)S(1)}, u32[]{:S(2)}, u32[]{:S(2)}) collective-permute-start(bf16[1,192,768]{2,1,0:T(8,128)(2,1)S(1)} %get-tuple-element.124), channel_id=1, source_target_pairs={{0,4},{1,5},{2,6},{3,7},{4,0},{5,1},{6,2},{7,3},{8,12},{9,13},{10,... | collective-permute-start | bytes 884744 | tf_op jit(solution)/shard_map/ppermute | solution.py:24
  169.6 17.9 %collective-permute-start.25 = (bf16[1,192,768]{2,1,0:T(8,128)(2,1)S(1)}, bf16[1,192,768]{2,1,0:T(8,128)(2,1)S(1)}, u32[]{:S(2)}, u32[]{:S(2)}) collective-permute-start(bf16[1,192,768]{2,1,0:T(8,128)(2,1)S(1)} %get-tuple-element.125), channel_id=1, source_target_pairs={{0,2},{1,3},{2,0},{3,1},{4,6},{5,7},{6,4},{7,5},{8,10},{9,11},{10,... | collective-permute-start | bytes 884744 | tf_op jit(solution)/shard_map/ppermute | solution.py:24
  194.5 17.4 %collective-permute-start.32 = (bf16[4,192,384]{2,1,0:T(8,128)(2,1)S(1)}, bf16[4,192,384]{2,1,0:T(8,128)(2,1)S(1)}, u32[]{:S(2)}, u32[]{:S(2)}) collective-permute-start(bf16[4,192,384]{2,1,0:T(8,128)(2,1)S(1)} %pad_maximum_fusion.9), channel_id=1, source_target_pairs={{0,4},{1,5},{2,6},{3,7},{4,0},{5,1},{6,2},{7,3},{8,12},{9,13},{10,... | collective-permute-start | bytes 1769480 | tf_op jit(solution)/shard_map/ppermute | solution.py:24
  198.3 15.1 %collective-permute-start.31 = (bf16[4,192,384]{2,1,0:T(8,128)(2,1)S(1)}, bf16[4,192,384]{2,1,0:T(8,128)(2,1)S(1)}, u32[]{:S(2)}, u32[]{:S(2)}) collective-permute-start(bf16[4,192,384]{2,1,0:T(8,128)(2,1)S(1)} %pad_maximum_fusion.9), channel_id=1, source_target_pairs={{0,2},{1,3},{2,0},{3,1},{4,6},{5,7},{6,4},{7,5},{8,10},{9,11},{10,... | collective-permute-start | bytes 1769480 | tf_op jit(solution)/shard_map/ppermute | solution.py:24
  213.5 19.4 %collective-permute-start.34 = (bf16[4,128,384]{2,1,0:T(8,128)(2,1)S(1)}, bf16[4,128,384]{2,1,0:T(8,128)(2,1)S(1)}, u32[]{:S(2)}, u32[]{:S(2)}) collective-permute-start(bf16[4,128,384]{2,1,0:T(8,128)(2,1)S(1)} %add_convert_fusion.1), channel_id=1, source_target_pairs={{0,16},{8,24},{16,0},{24,8},{1,17},{9,25},{17,1},{25,9},{2,18},{10... | collective-permute-start | bytes 1179656 | tf_op jit(solution)/shard_map/ppermute | solution.py:24
  213.6 19.4 %collective-permute-start.33 = (bf16[4,128,384]{2,1,0:T(8,128)(2,1)S(1)}, bf16[4,128,384]{2,1,0:T(8,128)(2,1)S(1)}, u32[]{:S(2)}, u32[]{:S(2)}) collective-permute-start(bf16[4,128,384]{2,1,0:T(8,128)(2,1)S(1)} %get-tuple-element.69), channel_id=1, source_target_pairs={{0,8},{8,0},{16,24},{24,16},{1,9},{9,1},{17,25},{25,17},{2,10},{10... | collective-permute-start | bytes 1179656 | tf_op jit(solution)/shard_map/ppermute | solution.py:24
  215.4 17.6 %collective-permute-start.35 = (bf16[4,192,384]{2,1,0:T(8,128)(2,1)S(1)}, bf16[4,192,384]{2,1,0:T(8,128)(2,1)S(1)}, u32[]{:S(2)}, u32[]{:S(2)}) collective-permute-start(bf16[4,192,384]{2,1,0:T(8,128)(2,1)S(1)} %pad_maximum_fusion.9), channel_id=1, source_target_pairs={{0,6},{1,7},{2,4},{3,5},{4,2},{5,3},{6,0},{7,1},{8,14},{9,15},{10,... | collective-permute-start | bytes 1769480 | tf_op jit(solution)/shard_map/ppermute | solution.py:24
  234.0 21.2 %collective-permute-start.38 = (bf16[4,128,384]{2,1,0:T(8,128)(2,1)S(1)}, bf16[4,128,384]{2,1,0:T(8,128)(2,1)S(1)}, u32[]{:S(2)}, u32[]{:S(2)}) collective-permute-start(bf16[4,128,384]{2,1,0:T(8,128)(2,1)S(1)} %pad_maximum_fusion.11), channel_id=1, source_target_pairs={{0,6},{1,7},{2,4},{3,5},{4,2},{5,3},{6,0},{7,1},{8,14},{9,15},{10,... | collective-permute-start | bytes 1179656 | tf_op jit(solution)/shard_map/ppermute | solution.py:24
  236.3 18.8 %collective-permute-start.37 = (bf16[4,128,384]{2,1,0:T(8,128)(2,1)S(1)}, bf16[4,128,384]{2,1,0:T(8,128)(2,1)S(1)}, u32[]{:S(2)}, u32[]{:S(2)}) collective-permute-start(bf16[4,128,384]{2,1,0:T(8,128)(2,1)S(1)} %pad_maximum_fusion.11), channel_id=1, source_target_pairs={{0,4},{1,5},{2,6},{3,7},{4,0},{5,1},{6,2},{7,3},{8,12},{9,13},{10,... | collective-permute-start | bytes 1179656 | tf_op jit(solution)/shard_map/ppermute | solution.py:24
  236.7 18.3 %collective-permute-start.36 = (bf16[4,128,384]{2,1,0:T(8,128)(2,1)S(1)}, bf16[4,128,384]{2,1,0:T(8,128)(2,1)S(1)}, u32[]{:S(2)}, u32[]{:S(2)}) collective-permute-start(bf16[4,128,384]{2,1,0:T(8,128)(2,1)S(1)} %pad_maximum_fusion.11), channel_id=1, source_target_pairs={{0,2},{1,3},{2,0},{3,1},{4,6},{5,7},{6,4},{7,5},{8,10},{9,11},{10,... | collective-permute-start | bytes 1179656 | tf_op jit(solution)/shard_map/ppermute | solution.py:24
  240.9 18.7 %collective-permute-start.40 = (bf16[3,192,384]{2,1,0:T(8,128)(2,1)S(1)}, bf16[3,192,384]{2,1,0:T(8,128)(2,1)S(1)}, u32[]{:S(2)}, u32[]{:S(2)}) collective-permute-start(bf16[3,192,384]{2,1,0:T(8,128)(2,1)S(1)} %dynamic-slice_convert_fusion), channel_id=1, source_target_pairs={{0,1},{1,0},{2,3},{3,2},{4,5},{5,4},{6,7},{7,6},{8,9},{9,8},{10,11... | collective-permute-start | bytes 1327112 | tf_op jit(solution)/shard_map/ppermute | solution.py:24
  (47 other events, 335.8 us)

commit v3 on v2

--- a/solution.py
+++ b/solution.py
@@ -111,26 +111,22 @@
     )
 
 
-def chip_sum(parts, ordered):
-    chips = lax.axis_size("seq") // 2
+def chip_sums(part, ordered):
+    chips, chip = lax.axis_size("seq") // 2, lax.axis_index("seq") // 2
     core, layer = lax.axis_index("seq") % 2, lax.axis_index("dp")
-    rows = parts[0].shape[0] // (2 * chips)
-    width = parts[0].shape[0] // lax.axis_size("dp")
-
-    def block(kind, chip):
-        offset = (2 * chip + kind) * rows
+    rows = part.shape[0] // (2 * chips)
+    width = part.shape[0] // lax.axis_size("dp")
+
+    def block(kind, target):
+        offset = (2 * target + kind) * rows
         if ordered:
             offset = ((offset // width) ^ layer) * width + offset % width
-        return jnp.stack([lax.dynamic_slice_in_dim(part, offset, rows, 0) for part in parts])
-
-    given = jnp.stack([block(1 - core, chip) for chip in range(chips)])
-    kept = jnp.stack([block(core, chip) for chip in range(chips)])
-    return (kept.astype(F32) + swap(given, "seq", 1).astype(F32)).astype(BF16)
-
-
-def chip_blocks(blocks):
-    chip = lax.axis_index("seq") // 2
-    return [lax.dynamic_index_in_dim(blocks, chip ^ j, 0, False) for j in range(blocks.shape[0])]
+        return lax.dynamic_slice_in_dim(part, offset, rows, 0)
+
+    return [
+        (block(core, chip ^ j).astype(F32) + swap(block(1 - core, chip ^ j), "seq", 1).astype(F32)).astype(BF16)
+        for j in range(chips)
+    ]
 
 
 def spread(chosen, steps):
@@ -207,17 +203,20 @@
     hidden_one, framed_in = tied(hidden_one, framed_in)
     in_blocks = channel_blocks(framed_in, False)
     early, late, _ = line_gather(hidden_one)
-    rows_one = jnp.concatenate(early + [late], axis=2)
-    rows_one, in_blocks[:-1] = tied(rows_one, in_blocks[:-1])
-    pre_two = conv_edges(rows_one, conv_two_r, second_gap)
+    early = jnp.concatenate(early, axis=2)
+    known = early.shape[2]
+    late, in_blocks[:-1] = tied(late, in_blocks[:-1])
+    pre_two = conv_edges(early, conv_two_r[:, :, :known], second_gap)
+    pre_two = pre_two + taps_sum(with_halo(late), conv_two_r[:, :, known:], second_gap, 1, "blc,dc->bld")
+    rows_one = jnp.concatenate([early, late], axis=2)
     hidden_two = (hidden_one.astype(F32) + activate(pre_two)).astype(BF16)
 
     hidden_two, rows_one, in_blocks[-1] = tied(hidden_two, rows_one, in_blocks[-1])
     one_blocks = channel_blocks(rows_one, True)
-    early, late, _ = line_gather(hidden_two)
-    rows_two = jnp.concatenate(early + [late], axis=2)
-    rows_two, one_blocks[:-1] = tied(rows_two, one_blocks[:-1])
-    logits = dot("blc,ct->blt", rows_two, head_r)
+    early, late, one_blocks[:-1] = line_gather(hidden_two, one_blocks[:-1])
+    early = jnp.concatenate(early, axis=2)
+    rows_two = jnp.concatenate([early, late], axis=2)
+    logits = dot("blc,ct->blt", early, head_r[:known]) + dot("blc,ct->blt", late, head_r[known:])
     peak = jnp.max(logits, axis=1)
     total = jnp.sum(jnp.exp(logits - peak[:, None, :]), axis=1)
     cross = jnp.sum(targets * logits, axis=1)
@@ -237,7 +236,7 @@
     back = dot("blt,ct->blc", logit_grad, head_r).astype(BF16)
     logit_grad, back = tied(logit_grad, back)
     head_part = dot("blc,blt->ct", rows_two, logit_grad).astype(BF16)
-    head_blocks = chip_blocks(chip_sum([head_part], True))
+    head_blocks = chip_sums(head_part, True)
     near_steps, far_steps = range(1, len(head_blocks) - 1), range(len(head_blocks) - 1, len(head_blocks))
     head_near, head_far = spread(head_blocks, near_steps), spread(head_blocks, far_steps)
     grad_two_out, _ = line_scatter(jnp.split(back, size, axis=2))
@@ -247,7 +246,7 @@
     framed_back = with_halo(up_two)
     back = taps_sum(framed_back, conv_two_r, second_gap, -1, "bld,dc->blc").astype(BF16)
     framed_back, back, head_far = tied(framed_back, back, head_far)
-    grad_head = total_of(head_blocks[:1] + head_near + head_far)[0]
+    grad_head = total_of(head_blocks[:1] + head_near + head_far)
     back_blocks = bin_blocks(framed_back)
     summed, back_blocks[:-1] = line_scatter(jnp.split(back, size, axis=2), back_blocks[:-1])
     summed, back_blocks[-1] = tied(summed, back_blocks[-1])

time: 262 us -> 244 us (0.931)
  waiting for transfers between devices: 111 us -> 100 us
  other arithmetic: 16.3 us -> 10.4 us
  local copies, waits for them, and re-layouts: 15.7 us -> 10.3 us
    ppermute x41 -> x46, waiting for transfers between devices: 111 us -> 100 us  [send(): return lax.ppermute(value, axis, pairs)]
    dynamic_slice x2, local copies, waits for them, and re-layouts: 4.19 us -> 0.96 us  [channel_blocks(): block = lax.dynamic_slice_in_dim(value, offset, wide, 2)]
    ppermute x41 -> x46, starting transfers between devices: 74 us -> 74.9 us  [send(): return lax.ppermute(value, axis, pairs)]
    dot_general x23 -> x27, matrix products: 25.2 us -> 25.5 us  [dot(): return jnp.einsum(spec, a, b, preferred_element_type=F32)]
  transfers between devices with their start and end apart: 41 -> 46, of which waited for: 19 -> 20; matrix products, arithmetic and copies ran while one was open for 17% -> 16% of each run, Pallas kernels for 0% -> 0%
where the time goes in v3:
time: 244 us
  waiting for transfers between devices  100 us (41%)
  starting transfers between devices  74.9 us (31%)
  matrix products  25.5 us (10%)
  blocking collectives  13.1 us (5%)
  other arithmetic  10.4 us (4%)
  local copies, waits for them, and re-layouts  10.3 us (4%)
  between operations  9.17 us (4%)
    ppermute x46, waiting for transfers between devices, send(): return lax.ppermute(value, axis, pairs)  100 us
    ppermute x46, starting transfers between devices, send(): return lax.ppermute(value, axis, pairs)  74.9 us
    dot_general x27, matrix products, dot(): return jnp.einsum(spec, a, b, preferred_element_type=F32)  25.5 us
    all_gather x1, blocking collectives, on_device(): lax.all_gather(jnp.stack([peak, total, jnp.sum(targets, axis=1), cross]),...  13.1 us
  transfers between devices with their start and end apart: 46, of which 20 were waited for; matrix products, arithmetic and copies ran while one was open for 16% of the time, Pallas kernels for 0%

profile of v3, /device:TPU:0, one launch (start us, length us, event | category | flops | bytes accessed | tf_op | source)
XLA Modules:
  0.0 243.7 jit_solution(12601311543501334716)
XLA Ops:
  0.6 4.1 %collective-permute-start = (bf16[1,128,1536]{2,1,0:T(8,128)(2,1)}, bf16[1,128,1536]{2,1,0:T(8,128)(2,1)S(1)}, u32[]{:S(2)}, u32[]{:S(2)}) collective-permute-start(bf16[1,128,1536]{2,1,0:T(8,128)(2,1)} %param.6), channel_id=1, source_target_pairs={{0,16},{8,24},{16,0},{24,8},{1,17},{9,25},{17,1},{25,9},{2,18},{10... | collective-permute-start | bytes 1179656 | tf_op jit(solution)/shard_map/ppermute | solution.py:24
  7.4 3.6 %constant_dynamic-slice_fusion.17 = (bf16[3,384,384]{2,1,0:T(8,128)(2,1)}, bf16[3,384,384]{2,1,0:T(8,128)(2,1)S(1)}, bf16[3,384,384]{2,1,0:T(8,128)(2,1)S(1)}, bf16[3,384,384]{2,1,0:T(8,128)(2,1)}) fusion(bf16[3,384,1536]{2,1,0:T(8,128)(2,1)} %param.8, s32[]{:T(128)S(6)} %select_n.364, s32[]{:T(128)S(6)} %select_n.346, s32[]{:T(128)S(6)} %select_n.327, ...), kind=kLoop, calls=%fused_computation.278 | loop fusion | bytes 7077904 | tf_op jit(solution)/shard_map/dynamic_slice | solution.py:109
  26.2 2.9 %collective-permute-start.3 = (bf16[3,32,1536]{2,1,0:T(8,128)(2,1)S(1)}, bf16[3,32,1536]{2,1,0:T(8,128)(2,1)S(1)}, u32[]{:S(2)}, u32[]{:S(2)}) collective-permute-start(bf16[3,32,1536]{2,1,0:T(8,128)(2,1)S(1)} %get-tuple-element.121), channel_id=1, source_target_pairs={{0,1},{1,0},{2,3},{3,2},{4,5},{5,4},{6,7},{7,6},{8,9},{9,8},{10,11... | collective-permute-start | bytes 884744 | tf_op jit(solution)/shard_map/ppermute | solution.py:24
  33.5 5.1 %collective-permute-start.6 = (bf16[1,32,1536]{2,1,0:T(8,128)(2,1)S(1)}, bf16[1,32,1536]{2,1,0:T(8,128)(2,1)S(1)}, u32[]{:S(2)}, u32[]{:S(2)}) collective-permute-start(bf16[1,32,1536]{2,1,0:T(8,128)(2,1)S(1)} %get-tuple-element.137), channel_id=1, source_target_pairs={{0,1},{1,0},{2,3},{3,2},{4,5},{5,4},{6,7},{7,6},{8,9},{9,8},{10,11... | collective-permute-start | bytes 294920 | tf_op jit(solution)/shard_map/ppermute | solution.py:24
  44.9 4.0 %collective-permute-start.12 = (bf16[4,192,384]{2,1,0:T(8,128)(2,1)S(1)}, bf16[4,192,384]{2,1,0:T(8,128)(2,1)S(1)}, u32[]{:S(2)}, u32[]{:S(2)}) collective-permute-start(bf16[4,192,384]{2,1,0:T(8,128)(2,1)S(1)} %get-tuple-element.110), channel_id=1, source_target_pairs={{0,2},{1,3},{2,0},{3,1},{4,6},{5,7},{6,4},{7,5},{8,10},{9,11},{10,... | collective-permute-start | bytes 1769480 | tf_op jit(solution)/shard_map/ppermute | solution.py:24
  48.9 2.9 %collective-permute-start.13 = (bf16[4,192,384]{2,1,0:T(8,128)(2,1)S(1)}, bf16[4,192,384]{2,1,0:T(8,128)(2,1)S(1)}, u32[]{:S(2)}, u32[]{:S(2)}) collective-permute-start(bf16[4,192,384]{2,1,0:T(8,128)(2,1)S(1)} %get-tuple-element.109), channel_id=1, source_target_pairs={{0,4},{1,5},{2,6},{3,7},{4,0},{5,1},{6,2},{7,3},{8,12},{9,13},{10,... | collective-permute-start | bytes 1769480 | tf_op jit(solution)/shard_map/ppermute | solution.py:24
  51.8 11.4 %collective-permute-done.7 = bf16[4,128,384]{2,1,0:T(8,128)(2,1)S(1)} collective-permute-done((bf16[4,128,384]{2,1,0:T(8,128)(2,1)S(1)}, bf16[4,128,384]{2,1,0:T(8,128)(2,1)S(1)}, u32[]{:S(2)}, u32[]{:S(2)}) %collective-permute-start.7) | collective-permute-done | bytes 393248 | tf_op jit(solution)/shard_map/ppermute | solution.py:24
  64.9 5.5 %collective-permute-start.10 = (bf16[4,32,384]{2,1,0:T(8,128)(2,1)S(1)}, bf16[4,32,384]{2,1,0:T(8,128)(2,1)S(1)}, u32[]{:S(2)}, u32[]{:S(2)}) collective-permute-start(bf16[4,32,384]{2,1,0:T(8,128)(2,1)S(1)} %get-tuple-element.143), channel_id=1, source_target_pairs={{0,1},{1,0},{2,3},{3,2},{4,5},{5,4},{6,7},{7,6},{8,9},{9,8},{10,11... | collective-permute-start | bytes 294920 | tf_op jit(solution)/shard_map/ppermute | solution.py:24
  76.0 5.7 %collective-permute-start.15 = (bf16[4,32,384]{2,1,0:T(8,128)(2,1)S(1)}, bf16[4,32,384]{2,1,0:T(8,128)(2,1)S(1)}, u32[]{:S(2)}, u32[]{:S(2)}) collective-permute-start(bf16[4,32,384]{2,1,0:T(8,128)(2,1)S(1)} %get-tuple-element.131), channel_id=1, source_target_pairs={{0,1},{1,0},{2,3},{3,2},{4,5},{5,4},{6,7},{7,6},{8,9},{9,8},{10,11... | collective-permute-start | bytes 294920 | tf_op jit(solution)/shard_map/ppermute | solution.py:24
  91.6 6.4 %collective-permute-start.19 = (bf16[4,128,384]{2,1,0:T(8,128)(2,1)S(1)}, bf16[4,128,384]{2,1,0:T(8,128)(2,1)S(1)}, u32[]{:S(2)}, u32[]{:S(2)}) collective-permute-start(bf16[4,128,384]{2,1,0:T(8,128)(2,1)S(1)} %get-tuple-element.118), channel_id=1, source_target_pairs={{0,2},{1,3},{2,0},{3,1},{4,6},{5,7},{6,4},{7,5},{8,10},{9,11},{10,... | collective-permute-start | bytes 1179656 | tf_op jit(solution)/shard_map/ppermute | solution.py:24
  98.0 3.5 %collective-permute-start.20 = (bf16[4,128,384]{2,1,0:T(8,128)(2,1)S(1)}, bf16[4,128,384]{2,1,0:T(8,128)(2,1)S(1)}, u32[]{:S(2)}, u32[]{:S(2)}) collective-permute-start(bf16[4,128,384]{2,1,0:T(8,128)(2,1)S(1)} %get-tuple-element.117), channel_id=1, source_target_pairs={{0,4},{1,5},{2,6},{3,7},{4,0},{5,1},{6,2},{7,3},{8,12},{9,13},{10,... | collective-permute-start | bytes 1179656 | tf_op jit(solution)/shard_map/ppermute | solution.py:24
  101.9 6.9 %collective-permute-done.17 = bf16[4,128,384]{2,1,0:T(8,128)(2,1)S(1)} collective-permute-done((bf16[4,128,384]{2,1,0:T(8,128)(2,1)S(1)}, bf16[4,128,384]{2,1,0:T(8,128)(2,1)S(1)}, u32[]{:S(2)}, u32[]{:S(2)}) %collective-permute-start.17) | collective-permute-done | bytes 393248 | tf_op jit(solution)/shard_map/ppermute | solution.py:24
  113.8 8.6 %collective-permute-done.21 = bf16[4,128,384]{2,1,0:T(8,128)(2,1)S(1)} collective-permute-done((bf16[4,128,384]{2,1,0:T(8,128)(2,1)S(1)}, bf16[4,128,384]{2,1,0:T(8,128)(2,1)S(1)}, u32[]{:S(2)}, u32[]{:S(2)}) %collective-permute-start.21) | collective-permute-done | bytes 393248 | tf_op jit(solution)/shard_map/ppermute | solution.py:24
  124.4 13.1 %all-gather = f32[32,4,768]{2,1,0:T(4,128)S(1)} all-gather(f32[4,4,768]{2,1,0:T(4,128)S(1)} %pad_maximum_fusion.12), channel_id=2, replica_groups=mesh['dp'=4,'seq'=8] {'seq'}, dimensions={0}, use_global_device_ids=true | all-gather | bytes 442368 | tf_op jit(solution)/shard_map/all_gather | solution.py:223
  143.1 8.6 %collective-permute-done.24 = bf16[4,128,384]{2,1,0:T(8,128)(2,1)S(1)} collective-permute-done((bf16[4,128,384]{2,1,0:T(8,128)(2,1)S(1)}, bf16[4,128,384]{2,1,0:T(8,128)(2,1)S(1)}, u32[]{:S(2)}, u32[]{:S(2)}) %collective-permute-start.24) | collective-permute-done | bytes 393248 | tf_op jit(solution)/shard_map/ppermute | solution.py:24
  158.1 13.6 %collective-permute-done.26 = bf16[4,128,384]{2,1,0:T(8,128)(2,1)S(1)} collective-permute-done((bf16[4,128,384]{2,1,0:T(8,128)(2,1)S(1)}, bf16[4,128,384]{2,1,0:T(8,128)(2,1)S(1)}, u32[]{:S(2)}, u32[]{:S(2)}) %collective-permute-start.26) | collective-permute-done | bytes 393248 | tf_op jit(solution)/shard_map/ppermute | solution.py:24
  178.1 2.7 %collective-permute-start.36 = (bf16[4,192,384]{2,1,0:T(8,128)(2,1)S(1)}, bf16[4,192,384]{2,1,0:T(8,128)(2,1)S(1)}, u32[]{:S(2)}, u32[]{:S(2)}) collective-permute-start(bf16[4,192,384]{2,1,0:T(8,128)(2,1)S(1)} %pad_maximum_fusion.9), channel_id=1, source_target_pairs={{0,2},{1,3},{2,0},{3,1},{4,6},{5,7},{6,4},{7,5},{8,10},{9,11},{10,... | collective-permute-start | bytes 1769480 | tf_op jit(solution)/shard_map/ppermute | solution.py:24
  180.9 2.6 %collective-permute-start.37 = (bf16[4,192,384]{2,1,0:T(8,128)(2,1)S(1)}, bf16[4,192,384]{2,1,0:T(8,128)(2,1)S(1)}, u32[]{:S(2)}, u32[]{:S(2)}) collective-permute-start(bf16[4,192,384]{2,1,0:T(8,128)(2,1)S(1)} %pad_maximum_fusion.9), channel_id=1, source_target_pairs={{0,4},{1,5},{2,6},{3,7},{4,0},{5,1},{6,2},{7,3},{8,12},{9,13},{10,... | collective-permute-start | bytes 1769480 | tf_op jit(solution)/shard_map/ppermute | solution.py:24
  184.0 9.3 %collective-permute-done.35 = bf16[4,128,384]{2,1,0:T(8,128)(2,1)S(1)} collective-permute-done((bf16[4,128,384]{2,1,0:T(8,128)(2,1)S(1)}, bf16[4,128,384]{2,1,0:T(8,128)(2,1)S(1)}, u32[]{:S(2)}, u32[]{:S(2)}) %collective-permute-start.35) | collective-permute-done | bytes 393248 | tf_op jit(solution)/shard_map/ppermute | solution.py:24
  194.0 3.4 %collective-permute-done.37 = bf16[4,192,384]{2,1,0:T(8,128)(2,1)S(1)} collective-permute-done((bf16[4,192,384]{2,1,0:T(8,128)(2,1)S(1)}, bf16[4,192,384]{2,1,0:T(8,128)(2,1)S(1)}, u32[]{:S(2)}, u32[]{:S(2)}) %collective-permute-start.37) | collective-permute-done | bytes 589856 | tf_op jit(solution)/shard_map/ppermute | solution.py:24
  200.5 15.8 %collective-permute-done.39 = bf16[4,128,384]{2,1,0:T(8,128)(2,1)S(1)} collective-permute-done((bf16[4,128,384]{2,1,0:T(8,128)(2,1)S(1)}, bf16[4,128,384]{2,1,0:T(8,128)(2,1)S(1)}, u32[]{:S(2)}, u32[]{:S(2)}) %collective-permute-start.39) | collective-permute-done | bytes 393248 | tf_op jit(solution)/shard_map/ppermute | solution.py:24
  218.7 2.9 %collective-permute-start.43 = (bf16[4,128,384]{2,1,0:T(8,128)(2,1)S(1)}, bf16[4,128,384]{2,1,0:T(8,128)(2,1)S(1)}, u32[]{:S(2)}, u32[]{:S(2)}) collective-permute-start(bf16[4,128,384]{2,1,0:T(8,128)(2,1)S(1)} %pad_maximum_fusion.11), channel_id=1, source_target_pairs={{0,6},{1,7},{2,4},{3,5},{4,2},{5,3},{6,0},{7,1},{8,14},{9,15},{10,... | collective-permute-start | bytes 1179656 | tf_op jit(solution)/shard_map/ppermute | solution.py:24
  225.1 5.2 %collective-permute-done.41 = bf16[4,128,384]{2,1,0:T(8,128)(2,1)S(1)} collective-permute-done((bf16[4,128,384]{2,1,0:T(8,128)(2,1)S(1)}, bf16[4,128,384]{2,1,0:T(8,128)(2,1)S(1)}, u32[]{:S(2)}, u32[]{:S(2)}) %collective-permute-start.41) | collective-permute-done | bytes 393248 | tf_op jit(solution)/shard_map/ppermute | solution.py:24
  230.3 6.8 %collective-permute-done.42 = bf16[4,128,384]{2,1,0:T(8,128)(2,1)S(1)} collective-permute-done((bf16[4,128,384]{2,1,0:T(8,128)(2,1)S(1)}, bf16[4,128,384]{2,1,0:T(8,128)(2,1)S(1)}, u32[]{:S(2)}, u32[]{:S(2)}) %collective-permute-start.42) | collective-permute-done | bytes 393248 | tf_op jit(solution)/shard_map/ppermute | solution.py:24
  (182 shorter events, 79.6 us)
Async XLA Ops:
  0.6 22.0 %collective-permute-start = (bf16[1,128,1536]{2,1,0:T(8,128)(2,1)}, bf16[1,128,1536]{2,1,0:T(8,128)(2,1)S(1)}, u32[]{:S(2)}, u32[]{:S(2)}) collective-permute-start(bf16[1,128,1536]{2,1,0:T(8,128)(2,1)} %param.6), channel_id=1, source_target_pairs={{0,16},{8,24},{16,0},{24,8},{1,17},{9,25},{17,1},{25,9},{2,18},{10... | collective-permute-start | bytes 1179656 | tf_op jit(solution)/shard_map/ppermute | solution.py:24
  4.7 18.2 %collective-permute-start.1 = (bf16[1,128,1536]{2,1,0:T(8,128)(2,1)}, bf16[1,128,1536]{2,1,0:T(8,128)(2,1)}, u32[]{:S(2)}, u32[]{:S(2)}) collective-permute-start(bf16[1,128,1536]{2,1,0:T(8,128)(2,1)} %param.6), channel_id=1, source_target_pairs={{0,8},{8,0},{16,24},{24,16},{1,9},{9,1},{17,25},{25,17},{2,10},{10... | collective-permute-start | bytes 1179656 | tf_op jit(solution)/shard_map/ppermute | solution.py:24
  41.9 21.4 %collective-permute-start.7 = (bf16[4,128,384]{2,1,0:T(8,128)(2,1)S(1)}, bf16[4,128,384]{2,1,0:T(8,128)(2,1)S(1)}, u32[]{:S(2)}, u32[]{:S(2)}) collective-permute-start(bf16[4,128,384]{2,1,0:T(8,128)(2,1)S(1)} %pad_maximum_fusion.10), channel_id=1, source_target_pairs={{0,16},{8,24},{16,0},{24,8},{1,17},{9,25},{17,1},{25,9},{2,18},{10... | collective-permute-start | bytes 1179656 | tf_op jit(solution)/shard_map/ppermute | solution.py:24
  44.2 19.1 %collective-permute-start.8 = (bf16[4,128,384]{2,1,0:T(8,128)(2,1)S(1)}, bf16[4,128,384]{2,1,0:T(8,128)(2,1)S(1)}, u32[]{:S(2)}, u32[]{:S(2)}) collective-permute-start(bf16[4,128,384]{2,1,0:T(8,128)(2,1)S(1)} %pad_maximum_fusion.10), channel_id=1, source_target_pairs={{0,8},{8,0},{16,24},{24,16},{1,9},{9,1},{17,25},{25,17},{2,10},{10... | collective-permute-start | bytes 1179656 | tf_op jit(solution)/shard_map/ppermute | solution.py:24
  44.9 29.5 %collective-permute-start.12 = (bf16[4,192,384]{2,1,0:T(8,128)(2,1)S(1)}, bf16[4,192,384]{2,1,0:T(8,128)(2,1)S(1)}, u32[]{:S(2)}, u32[]{:S(2)}) collective-permute-start(bf16[4,192,384]{2,1,0:T(8,128)(2,1)S(1)} %get-tuple-element.110), channel_id=1, source_target_pairs={{0,2},{1,3},{2,0},{3,1},{4,6},{5,7},{6,4},{7,5},{8,10},{9,11},{10,... | collective-permute-start | bytes 1769480 | tf_op jit(solution)/shard_map/ppermute | solution.py:24
  48.9 25.5 %collective-permute-start.13 = (bf16[4,192,384]{2,1,0:T(8,128)(2,1)S(1)}, bf16[4,192,384]{2,1,0:T(8,128)(2,1)S(1)}, u32[]{:S(2)}, u32[]{:S(2)}) collective-permute-start(bf16[4,192,384]{2,1,0:T(8,128)(2,1)S(1)} %get-tuple-element.109), channel_id=1, source_target_pairs={{0,4},{1,5},{2,6},{3,7},{4,0},{5,1},{6,2},{7,3},{8,12},{9,13},{10,... | collective-permute-start | bytes 1769480 | tf_op jit(solution)/shard_map/ppermute | solution.py:24
  72.1 17.0 %collective-permute-start.16 = (bf16[4,192,384]{2,1,0:T(8,128)(2,1)S(1)}, bf16[4,192,384]{2,1,0:T(8,128)(2,1)S(1)}, u32[]{:S(2)}, u32[]{:S(2)}) collective-permute-start(bf16[4,192,384]{2,1,0:T(8,128)(2,1)S(1)} %get-tuple-element.108), channel_id=1, source_target_pairs={{0,6},{1,7},{2,4},{3,5},{4,2},{5,3},{6,0},{7,1},{8,14},{9,15},{10,... | collective-permute-start | bytes 1769480 | tf_op jit(solution)/shard_map/ppermute | solution.py:24
  89.0 19.8 %collective-permute-start.17 = (bf16[4,128,384]{2,1,0:T(8,128)(2,1)S(1)}, bf16[4,128,384]{2,1,0:T(8,128)(2,1)S(1)}, u32[]{:S(2)}, u32[]{:S(2)}) collective-permute-start(bf16[4,128,384]{2,1,0:T(8,128)(2,1)S(1)} %get-tuple-element.48), channel_id=1, source_target_pairs={{0,16},{8,24},{16,0},{24,8},{1,17},{9,25},{17,1},{25,9},{2,18},{10... | collective-permute-start | bytes 1179656 | tf_op jit(solution)/shard_map/ppermute | solution.py:24
  89.9 18.9 %collective-permute-start.18 = (bf16[4,128,384]{2,1,0:T(8,128)(2,1)S(1)}, bf16[4,128,384]{2,1,0:T(8,128)(2,1)S(1)}, u32[]{:S(2)}, u32[]{:S(2)}) collective-permute-start(bf16[4,128,384]{2,1,0:T(8,128)(2,1)S(1)} %get-tuple-element.48), channel_id=1, source_target_pairs={{0,8},{8,0},{16,24},{24,16},{1,9},{9,1},{17,25},{25,17},{2,10},{10... | collective-permute-start | bytes 1179656 | tf_op jit(solution)/shard_map/ppermute | solution.py:24
  91.6 17.2 %collective-permute-start.19 = (bf16[4,128,384]{2,1,0:T(8,128)(2,1)S(1)}, bf16[4,128,384]{2,1,0:T(8,128)(2,1)S(1)}, u32[]{:S(2)}, u32[]{:S(2)}) collective-permute-start(bf16[4,128,384]{2,1,0:T(8,128)(2,1)S(1)} %get-tuple-element.118), channel_id=1, source_target_pairs={{0,2},{1,3},{2,0},{3,1},{4,6},{5,7},{6,4},{7,5},{8,10},{9,11},{10,... | collective-permute-start | bytes 1179656 | tf_op jit(solution)/shard_map/ppermute | solution.py:24
  112.5 25.1 %collective-permute-start.22 = (bf16[4,128,384]{2,1,0:T(8,128)(2,1)S(1)}, bf16[4,128,384]{2,1,0:T(8,128)(2,1)S(1)}, u32[]{:S(2)}, u32[]{:S(2)}) collective-permute-start(bf16[4,128,384]{2,1,0:T(8,128)(2,1)S(1)} %get-tuple-element.116), channel_id=1, source_target_pairs={{0,6},{1,7},{2,4},{3,5},{4,2},{5,3},{6,0},{7,1},{8,14},{9,15},{10,... | collective-permute-start | bytes 1179656 | tf_op jit(solution)/shard_map/ppermute | solution.py:24
  151.8 20.0 %collective-permute-start.26 = (bf16[4,128,384]{2,1,0:T(8,128)(2,1)S(1)}, bf16[4,128,384]{2,1,0:T(8,128)(2,1)S(1)}, u32[]{:S(2)}, u32[]{:S(2)}) collective-permute-start(bf16[4,128,384]{2,1,0:T(8,128)(2,1)S(1)} %add_convert_fusion.1), channel_id=1, source_target_pairs={{0,16},{8,24},{16,0},{24,8},{1,17},{9,25},{17,1},{25,9},{2,18},{10... | collective-permute-start | bytes 1179656 | tf_op jit(solution)/shard_map/ppermute | solution.py:24
  153.2 18.7 %collective-permute-start.25 = (bf16[4,128,384]{2,1,0:T(8,128)(2,1)S(1)}, bf16[4,128,384]{2,1,0:T(8,128)(2,1)S(1)}, u32[]{:S(2)}, u32[]{:S(2)}) collective-permute-start(bf16[4,128,384]{2,1,0:T(8,128)(2,1)S(1)} %get-tuple-element.55), channel_id=1, source_target_pairs={{0,8},{8,0},{16,24},{24,16},{1,9},{9,1},{17,25},{25,17},{2,10},{10... | collective-permute-start | bytes 1179656 | tf_op jit(solution)/shard_map/ppermute | solution.py:24
  154.4 18.2 %collective-permute-start.28 = (bf16[192,768]{1,0:T(8,128)(2,1)S(1)}, bf16[192,768]{1,0:T(8,128)(2,1)S(1)}, u32[]{:S(2)}, u32[]{:S(2)}) collective-permute-start(bf16[192,768]{1,0:T(8,128)(2,1)S(1)} %get-tuple-element.103), channel_id=1, source_target_pairs={{0,2},{1,3},{2,0},{3,1},{4,6},{5,7},{6,4},{7,5},{8,10},{9,11},{10,... | collective-permute-start | bytes 884744 | tf_op jit(solution)/shard_map/ppermute | solution.py:24
  154.8 17.8 %collective-permute-start.30 = (bf16[192,768]{1,0:T(8,128)(2,1)S(1)}, bf16[192,768]{1,0:T(8,128)(2,1)S(1)}, u32[]{:S(2)}, u32[]{:S(2)}) collective-permute-start(bf16[192,768]{1,0:T(8,128)(2,1)S(1)} %get-tuple-element.102), channel_id=1, source_target_pairs={{0,4},{1,5},{2,6},{3,7},{4,0},{5,1},{6,2},{7,3},{8,12},{9,13},{10,... | collective-permute-start | bytes 884744 | tf_op jit(solution)/shard_map/ppermute | solution.py:24
  156.6 21.5 %collective-permute-start.34 = (bf16[192,768]{1,0:T(8,128)(2,1)S(1)}, bf16[192,768]{1,0:T(8,128)(2,1)S(1)}, u32[]{:S(2)}, u32[]{:S(2)}) collective-permute-start(bf16[192,768]{1,0:T(8,128)(2,1)S(1)} %get-tuple-element.101), channel_id=1, source_target_pairs={{0,6},{1,7},{2,4},{3,5},{4,2},{5,3},{6,0},{7,1},{8,14},{9,15},{10,... | collective-permute-start | bytes 884744 | tf_op jit(solution)/shard_map/ppermute | solution.py:24
  180.9 16.6 %collective-permute-start.37 = (bf16[4,192,384]{2,1,0:T(8,128)(2,1)S(1)}, bf16[4,192,384]{2,1,0:T(8,128)(2,1)S(1)}, u32[]{:S(2)}, u32[]{:S(2)}) collective-permute-start(bf16[4,192,384]{2,1,0:T(8,128)(2,1)S(1)} %pad_maximum_fusion.9), channel_id=1, source_target_pairs={{0,4},{1,5},{2,6},{3,7},{4,0},{5,1},{6,2},{7,3},{8,12},{9,13},{10,... | collective-permute-start | bytes 1769480 | tf_op jit(solution)/shard_map/ppermute | solution.py:24
  184.0 56.6 %collective-permute-start.23 = (bf16[192,768]{1,0:T(8,128)(2,1)S(1)}, bf16[192,768]{1,0:T(8,128)(2,1)S(1)}, u32[]{:S(2)}, u32[]{:S(2)}) collective-permute-start(bf16[192,768]{1,0:T(8,128)(2,1)S(1)} %get-tuple-element.97), channel_id=1, source_target_pairs={{0,1},{1,0},{2,3},{3,2},{4,5},{5,4},{6,7},{7,6},{8,9},{9,8},{10,11... | collective-permute-start | bytes 884744 | tf_op jit(solution)/shard_map/ppermute | solution.py:24
  197.6 18.7 %collective-permute-start.39 = (bf16[4,128,384]{2,1,0:T(8,128)(2,1)S(1)}, bf16[4,128,384]{2,1,0:T(8,128)(2,1)S(1)}, u32[]{:S(2)}, u32[]{:S(2)}) collective-permute-start(bf16[4,128,384]{2,1,0:T(8,128)(2,1)S(1)} %add_convert_fusion), channel_id=1, source_target_pairs={{0,16},{8,24},{16,0},{24,8},{1,17},{9,25},{17,1},{25,9},{2,18},{10... | collective-permute-start | bytes 1179656 | tf_op jit(solution)/shard_map/ppermute | solution.py:24
  197.6 19.4 %collective-permute-start.38 = (bf16[4,128,384]{2,1,0:T(8,128)(2,1)S(1)}, bf16[4,128,384]{2,1,0:T(8,128)(2,1)S(1)}, u32[]{:S(2)}, u32[]{:S(2)}) collective-permute-start(bf16[4,128,384]{2,1,0:T(8,128)(2,1)S(1)} %get-tuple-element.67), channel_id=1, source_target_pairs={{0,8},{8,0},{16,24},{24,16},{1,9},{9,1},{17,25},{25,17},{2,10},{10... | collective-permute-start | bytes 1179656 | tf_op jit(solution)/shard_map/ppermute | solution.py:24
  199.3 17.8 %collective-permute-start.40 = (bf16[4,192,384]{2,1,0:T(8,128)(2,1)S(1)}, bf16[4,192,384]{2,1,0:T(8,128)(2,1)S(1)}, u32[]{:S(2)}, u32[]{:S(2)}) collective-permute-start(bf16[4,192,384]{2,1,0:T(8,128)(2,1)S(1)} %pad_maximum_fusion.9), channel_id=1, source_target_pairs={{0,6},{1,7},{2,4},{3,5},{4,2},{5,3},{6,0},{7,1},{8,14},{9,15},{10,... | collective-permute-start | bytes 1769480 | tf_op jit(solution)/shard_map/ppermute | solution.py:24
  218.7 18.4 %collective-permute-start.42 = (bf16[4,128,384]{2,1,0:T(8,128)(2,1)S(1)}, bf16[4,128,384]{2,1,0:T(8,128)(2,1)S(1)}, u32[]{:S(2)}, u32[]{:S(2)}) collective-permute-start(bf16[4,128,384]{2,1,0:T(8,128)(2,1)S(1)} %pad_maximum_fusion.11), channel_id=1, source_target_pairs={{0,4},{1,5},{2,6},{3,7},{4,0},{5,1},{6,2},{7,3},{8,12},{9,13},{10,... | collective-permute-start | bytes 1179656 | tf_op jit(solution)/shard_map/ppermute | solution.py:24
  218.7 18.4 %collective-permute-start.43 = (bf16[4,128,384]{2,1,0:T(8,128)(2,1)S(1)}, bf16[4,128,384]{2,1,0:T(8,128)(2,1)S(1)}, u32[]{:S(2)}, u32[]{:S(2)}) collective-permute-start(bf16[4,128,384]{2,1,0:T(8,128)(2,1)S(1)} %pad_maximum_fusion.11), channel_id=1, source_target_pairs={{0,6},{1,7},{2,4},{3,5},{4,2},{5,3},{6,0},{7,1},{8,14},{9,15},{10,... | collective-permute-start | bytes 1179656 | tf_op jit(solution)/shard_map/ppermute | solution.py:24
  225.0 16.7 %collective-permute-start.45 = (bf16[3,192,384]{2,1,0:T(8,128)(2,1)S(1)}, bf16[3,192,384]{2,1,0:T(8,128)(2,1)S(1)}, u32[]{:S(2)}, u32[]{:S(2)}) collective-permute-start(bf16[3,192,384]{2,1,0:T(8,128)(2,1)S(1)} %dynamic-slice_convert_fusion), channel_id=1, source_target_pairs={{0,1},{1,0},{2,3},{3,2},{4,5},{5,4},{6,7},{7,6},{8,9},{9,8},{10,11... | collective-permute-start | bytes 1327112 | tf_op jit(solution)/shard_map/ppermute | solution.py:24
  (28 other events, 238.7 us)
